TPU v7x, 32 devices: a whole 2x2x4 slice. The times are simulated.
32 devices in a mesh: dp: 8 (over z, y), mp: 4 (over x, core).
Axes of the slice: x: 2, y: 2, z: 4, core: 2. Of those that a mesh axis runs over, the one named last changes fastest.
Arguments:
- tokens: bfloat16 [10240, 1024], P(('dp', 'mp')), may hold values from -6 to 6
- cond: bfloat16 [8, 1024], P('dp'), may hold values from -3 to 3
- pad_mask: int32 [8, 1280], P('dp'), may hold values from 0 to 1, as said below
- spatial_index: int32 [256, 256], replicated, may hold values from 0 to 960
- joint_index: int32 [320, 320], replicated, may hold values from 0 to 2024
- qkv_a: bfloat16 [1024, 3, 1024], P(None, None, 'mp'), may hold values from -0.1875 to 0.1875
- proj_a: bfloat16 [1024, 1024], P('mp'), may hold values from -0.75 to 0.75
- fc1_a: bfloat16 [1024, 4096], P(None, 'mp'), may hold values from -0.1875 to 0.1875
- fc2_a: bfloat16 [4096, 1024], P('mp'), may hold values from -0.09375 to 0.09375
- table_a: bfloat16 [961, 16], P(None, 'mp'), may hold values from -2.5 to 2.5
- ada_a: bfloat16 [1024, 6144], P(None, 'mp'), may hold values from -0.1875 to 0.1875
- qkv_b: bfloat16 [1024, 3, 1024], P(None, None, 'mp'), may hold values from -0.1875 to 0.1875
- proj_b: bfloat16 [1024, 1024], P('mp'), may hold values from -0.75 to 0.75
- fc1_b: bfloat16 [1024, 4096], P(None, 'mp'), may hold values from -0.1875 to 0.1875
- fc2_b: bfloat16 [4096, 1024], P('mp'), may hold values from -0.09375 to 0.09375
- table_b: bfloat16 [2025, 16], P(None, 'mp'), may hold values from -2.5 to 2.5
- ada_b: bfloat16 [1024, 6144], P(None, 'mp'), may hold values from -0.1875 to 0.1875
- cotangent: bfloat16 [10240, 1024], P(('dp', 'mp')), may hold values from -6 to 6
Outputs:
- output: float32 [10240, 1024], P(('dp', 'mp'))
- token_grad: float32 [10240, 1024], P(('dp', 'mp'))
- grad_qkv_a: float32 [1024, 3, 1024], P('dp', None, 'mp')
- grad_proj_a: float32 [1024, 1024], P('mp', 'dp')
- grad_fc1_a: float32 [1024, 4096], P('dp', 'mp')
- grad_fc2_a: float32 [4096, 1024], P('mp', 'dp')
- grad_table_a: float32 [961, 16], P(None, 'mp')
- grad_ada_a: float32 [1024, 6144], P('dp', 'mp')
- grad_qkv_b: float32 [1024, 3, 1024], P('dp', None, 'mp')
- grad_proj_b: float32 [1024, 1024], P('mp', 'dp')
- grad_fc1_b: float32 [1024, 4096], P('dp', 'mp')
- grad_fc2_b: float32 [4096, 1024], P('mp', 'dp')
- grad_table_b: float32 [2025, 16], P(None, 'mp')
- grad_ada_b: float32 [1024, 6144], P('dp', 'mp')
Inputs may be any that keep to these rules, and one draw needn't show every extreme that they name: `pad_mask`: in each tile the positions marked 1 are those whose row is below the tile's own height and whose column is below its own width, both from 9 to 16, the same in all frames; the first tile is always narrower than 16.
All inputs are finite; a program needn't handle non-finite values.
Results may differ from a plain program's by a relative error of at most 0.035.
The roundings to bfloat16 on the way count: a program that leaves them out, or rounds other values in their place, can miss the bound.
Values may be sent and summed in bfloat16 or wider, within the bound.
A program may use at most 256 MiB of HBM per device.

v0:
```python
import jax
import jax.numpy as jnp
from jax import lax
from jax.sharding import PartitionSpec as P

FRAMES = 5
SIDE = 16


EPSILON = 1e-06
HIGHEST = lax.Precision.HIGHEST
QUERY_BLOCK = 16


def layer_norm(values):
    average = jnp.mean(values, axis=-1, keepdims=True)
    centred = values - average
    return centred * lax.rsqrt(jnp.mean(centred * centred, axis=-1, keepdims=True) + EPSILON)


def norm_back(values, grad_out):
    return jax.vjp(layer_norm, values)[1](grad_out)[0]


def gelu_tanh(values):
    return jax.nn.gelu(values, approximate=True)


def to_windows(tensor, layout):
    trailing = tensor.shape[1:]
    tiles_here = tensor.shape[0] // (FRAMES * SIDE * SIDE)
    if layout == 0:
        return tensor.reshape((tiles_here * FRAMES, SIDE * SIDE) + trailing)
    half_side = SIDE // 2
    shaped = tensor.reshape((tiles_here, FRAMES, 2, half_side, 2, half_side) + trailing)
    ordering = (0, 2, 4, 1, 3, 5) + tuple(range(6, 6 + len(trailing)))
    return jnp.transpose(shaped, ordering).reshape(
        (tiles_here * 4, FRAMES * half_side * half_side) + trailing
    )


def from_windows(tensor, layout):
    trailing = tensor.shape[2:]
    if layout == 0:
        return tensor.reshape((-1,) + trailing)
    tiles_here = tensor.shape[0] // 4
    half_side = SIDE // 2
    shaped = tensor.reshape((tiles_here, 2, 2, FRAMES, half_side, half_side) + trailing)
    ordering = (0, 3, 1, 4, 2, 5) + tuple(range(6, 6 + len(trailing)))
    return jnp.transpose(shaped, ordering).reshape((-1,) + trailing)


def bias_lookup(bias_table, rel_index):
    width = rel_index.shape[0]
    blocks = rel_index.reshape(width // QUERY_BLOCK, QUERY_BLOCK * width)
    table_rows = jnp.arange(bias_table.shape[0], dtype=jnp.int32)

    def bias_one_block(indices):
        onehot = (indices[:, None] == table_rows[None, :]).astype(jnp.bfloat16)
        return jnp.dot(onehot, bias_table, preferred_element_type=jnp.float32)

    looked = lax.map(bias_one_block, blocks)
    return jnp.transpose(looked.reshape(width, width, -1), (2, 0, 1))


def table_scatter(grad_bias, rel_index, table_len):
    width = rel_index.shape[0]
    heads_here = grad_bias.shape[-1]
    blocks = rel_index.reshape(width // QUERY_BLOCK, QUERY_BLOCK * width)
    grad_blocks = grad_bias.reshape(width // QUERY_BLOCK, QUERY_BLOCK * width, heads_here)
    table_rows = jnp.arange(table_len, dtype=jnp.int32)

    def table_one_block(pieces):
        indices, grads = pieces
        onehot = (indices[:, None] == table_rows[None, :]).astype(jnp.float32)
        return jnp.einsum("rn,rh->nh", onehot, grads, precision=HIGHEST)

    return jnp.sum(lax.map(table_one_block, (blocks, grad_blocks)), axis=0)


def gather_rows(values):
    return lax.all_gather(values, "mp", axis=0, tiled=True)


def reduce_rows(values):
    return lax.psum_scatter(values, "mp", scatter_dimension=0, tiled=True)


def gather_grads(values):
    return lax.all_gather(values, "mp", axis=0, tiled=True)


def reduce_grads(values):
    return lax.psum_scatter(values, "mp", scatter_dimension=0, tiled=True)


def modulation(cond_act, ada_first, ada_second):
    part_first = jnp.dot(cond_act, ada_first, preferred_element_type=jnp.float32)
    part_second = jnp.dot(cond_act, ada_second, preferred_element_type=jnp.float32)
    whole_first, whole_second = (
        lax.all_gather(part_first, "mp", axis=1, tiled=True),
        lax.all_gather(part_second, "mp", axis=1, tiled=True),
    )
    return (
        whole_first.reshape(cond_act.shape[0], 6, -1),
        whole_second.reshape(cond_act.shape[0], 6, -1),
    )


def membership(local_rows, tiles_here):
    global_row = lax.axis_index("mp") * local_rows + jnp.arange(local_rows, dtype=jnp.int32)
    owner = global_row // (FRAMES * SIDE * SIDE)
    return (owner[:, None] == jnp.arange(tiles_here, dtype=jnp.int32)[None, :]).astype(jnp.float32)


def spread_rows(member, modulated):
    return jnp.einsum("lt,tsc->lsc", member, modulated, precision=HIGHEST)


def ada_grad(member, grad_mod, cond_act):
    per_tile = jnp.einsum("lt,lsc->tsc", member, grad_mod, precision=HIGHEST).reshape(
        member.shape[1], -1
    )
    columns = lax.psum_scatter(per_tile, "mp", scatter_dimension=1, tiled=True)
    return jnp.einsum("td,tc->dc", cond_act.astype(jnp.float32), columns, precision=HIGHEST)


def sum_block(grads, grad_ada):
    return (
        lax.psum_scatter(grads[0], "dp", scatter_dimension=0, tiled=True),
        lax.psum_scatter(grads[1], "dp", scatter_dimension=1, tiled=True),
        lax.psum_scatter(grads[2], "dp", scatter_dimension=0, tiled=True),
        lax.psum_scatter(grads[3], "dp", scatter_dimension=1, tiled=True),
        lax.psum_scatter(grad_ada, "dp", scatter_dimension=0, tiled=True),
    )


def window_scores(queries, keys_win, bias_table, rel_index, validity, layout, scale):
    biases = bias_lookup(bias_table, rel_index)
    scores = (
        jnp.einsum("wqhe,wkhe->whqk", queries, keys_win, preferred_element_type=jnp.float32) * scale
        + biases[None]
    )
    visible = to_windows(validity.reshape(-1), layout)[:, None, None, :] > 0
    return jnp.where(visible, scores, -1e30)


def attention_forward(gathered, qkv_w, bias_table, rel_index, validity, layout):
    rows_all = gathered.shape[0]
    heads_here = bias_table.shape[1]
    head_dim = qkv_w.shape[2] // heads_here
    projected = jnp.dot(
        gathered, qkv_w.reshape(qkv_w.shape[0], -1), preferred_element_type=jnp.float32
    )
    projected = projected.astype(jnp.bfloat16).reshape(rows_all, 3, heads_here, head_dim)
    queries = to_windows(projected[:, 0], layout)
    keys_win = to_windows(projected[:, 1], layout)
    values_win = to_windows(projected[:, 2], layout)
    scores = window_scores(
        queries, keys_win, bias_table, rel_index, validity, layout, head_dim ** (-0.5)
    )
    row_max = jnp.max(scores, axis=-1, keepdims=True)
    weights = jnp.exp(scores - row_max)
    totals = jnp.sum(weights, axis=-1, keepdims=True)
    attn_prob = (weights / totals).astype(jnp.bfloat16)
    log_total = row_max + jnp.log(totals)
    attended = jnp.einsum(
        "whqk,wkhe->wqhe", attn_prob, values_win, preferred_element_type=jnp.float32
    )
    attended = from_windows(attended, layout).reshape(rows_all, -1).astype(jnp.bfloat16)
    return (attended, (queries, keys_win, values_win, log_total))


def attention_backward(grad_attended, saved_attn, bias_table, rel_index, validity, layout):
    queries, keys_win, values_win, log_total = saved_attn
    rows_all = grad_attended.shape[0]
    heads_here = bias_table.shape[1]
    head_dim = queries.shape[-1]
    scale = head_dim ** (-0.5)
    grad_win = to_windows(grad_attended.reshape(rows_all, heads_here, head_dim), layout)
    scores = window_scores(queries, keys_win, bias_table, rel_index, validity, layout, scale)
    attn_prob = jnp.exp(scores - log_total)
    grad_prob = jnp.einsum(
        "wqhe,wkhe->whqk", grad_win, values_win, preferred_element_type=jnp.float32
    )
    grad_values = jnp.einsum(
        "whqk,wqhe->wkhe",
        attn_prob.astype(jnp.bfloat16),
        grad_win,
        preferred_element_type=jnp.float32,
    )
    row_dot = jnp.sum(attn_prob * grad_prob, axis=-1, keepdims=True)
    grad_scores = attn_prob * (grad_prob - row_dot)
    grad_bias = jnp.transpose(jnp.sum(grad_scores, axis=0), (1, 2, 0)).reshape(-1, heads_here)
    table_grad = table_scatter(grad_bias, rel_index, bias_table.shape[0])
    rounded = grad_scores.astype(jnp.bfloat16)
    grad_queries = (
        jnp.einsum("whqk,wkhe->wqhe", rounded, keys_win, preferred_element_type=jnp.float32) * scale
    )
    grad_keys = (
        jnp.einsum("whqk,wqhe->wkhe", rounded, queries, preferred_element_type=jnp.float32) * scale
    )
    stacked = jnp.stack(
        [
            from_windows(grad_queries, layout),
            from_windows(grad_keys, layout),
            from_windows(grad_values, layout),
        ],
        axis=1,
    )
    return (stacked.astype(jnp.bfloat16).reshape(rows_all, -1), table_grad)


def block_forward(stream, rows_mod, params, rel_index, validity, layout):
    qkv_w, proj_w, fc1_w, fc2_w, bias_table = params
    normed_one = layer_norm(stream)
    gathered_one = gather_rows(
        (normed_one * (1.0 + rows_mod[:, 1]) + rows_mod[:, 0]).astype(jnp.bfloat16)
    )
    attended, saved_attn = attention_forward(
        gathered_one, qkv_w, bias_table, rel_index, validity, layout
    )
    attn_out = reduce_rows(jnp.dot(attended, proj_w, preferred_element_type=jnp.float32))
    stream_mid = stream + rows_mod[:, 2] * attn_out
    normed_two = layer_norm(stream_mid)
    gathered_two = gather_rows(
        (normed_two * (1.0 + rows_mod[:, 4]) + rows_mod[:, 3]).astype(jnp.bfloat16)
    )
    hidden = jnp.dot(gathered_two, fc1_w, preferred_element_type=jnp.float32)
    activated = gelu_tanh(hidden).astype(jnp.bfloat16)
    mlp_out = reduce_rows(jnp.dot(activated, fc2_w, preferred_element_type=jnp.float32))
    result = stream_mid + rows_mod[:, 5] * mlp_out
    kept_acts = (
        normed_one,
        gathered_one,
        attended,
        saved_attn,
        attn_out,
        stream_mid,
        normed_two,
        gathered_two,
        hidden,
        activated,
        mlp_out,
    )
    return (result, kept_acts)


def block_backward(stream, grad_out, rows_mod, params, kept_acts, rel_index, validity, layout):
    qkv_w, proj_w, fc1_w, fc2_w, bias_table = params
    (
        normed_one,
        gathered_one,
        attended,
        saved_attn,
        attn_out,
        stream_mid,
        normed_two,
        gathered_two,
        hidden,
        activated,
        mlp_out,
    ) = kept_acts
    grad_mlp = gather_grads((rows_mod[:, 5] * grad_out).astype(jnp.bfloat16))
    grad_fc2 = jnp.einsum("gf,gd->fd", activated, grad_mlp, preferred_element_type=jnp.float32)
    grad_act = jnp.einsum("gd,fd->gf", grad_mlp, fc2_w, preferred_element_type=jnp.float32)
    grad_hidden = jax.vjp(gelu_tanh, hidden)[1](grad_act)[0].astype(jnp.bfloat16)
    grad_fc1 = jnp.einsum(
        "gd,gf->df", gathered_two, grad_hidden, preferred_element_type=jnp.float32
    )
    grad_normed_two = reduce_grads(
        jnp.einsum("gf,df->gd", grad_hidden, fc1_w, preferred_element_type=jnp.float32)
    )
    grad_mid = grad_out + norm_back(stream_mid, grad_normed_two * (1.0 + rows_mod[:, 4]))
    grad_attn = gather_grads((rows_mod[:, 2] * grad_mid).astype(jnp.bfloat16))
    grad_proj = jnp.einsum("gc,gd->cd", attended, grad_attn, preferred_element_type=jnp.float32)
    grad_attended = jnp.einsum(
        "gd,cd->gc", grad_attn, proj_w, preferred_element_type=jnp.float32
    ).astype(jnp.bfloat16)
    grad_qkv_rows, table_grad = attention_backward(
        grad_attended, saved_attn, bias_table, rel_index, validity, layout
    )
    qkv_flat = qkv_w.reshape(qkv_w.shape[0], -1)
    grad_qkv = jnp.einsum(
        "gd,gc->dc", gathered_one, grad_qkv_rows, preferred_element_type=jnp.float32
    ).reshape(qkv_w.shape)
    grad_normed_one = reduce_grads(
        jnp.einsum("gc,dc->gd", grad_qkv_rows, qkv_flat, preferred_element_type=jnp.float32)
    )
    grad_stream = grad_mid + norm_back(stream, grad_normed_one * (1.0 + rows_mod[:, 1]))
    grad_mod = jnp.stack(
        [
            grad_normed_one,
            grad_normed_one * normed_one,
            grad_mid * attn_out,
            grad_normed_two,
            grad_normed_two * normed_two,
            grad_out * mlp_out,
        ],
        axis=1,
    )
    return (grad_stream, grad_mod, (grad_qkv, grad_proj, grad_fc1, grad_fc2), table_grad)


def local(
    tokens,
    cond,
    pad_mask,
    spatial_index,
    joint_index,
    qkv_a,
    proj_a,
    fc1_a,
    fc2_a,
    table_a,
    ada_a,
    qkv_b,
    proj_b,
    fc1_b,
    fc2_b,
    table_b,
    ada_b,
    cotangent,
):
    stream_in = tokens.astype(jnp.float32)
    member = membership(stream_in.shape[0], cond.shape[0])
    cond_act = jax.nn.silu(cond.astype(jnp.float32)).astype(jnp.bfloat16)
    params_a = (qkv_a, proj_a, fc1_a, fc2_a, table_a)
    params_b = (qkv_b, proj_b, fc1_b, fc2_b, table_b)
    modulated_a, modulated_b = modulation(cond_act, ada_a, ada_b)
    rows_mod_a = spread_rows(member, modulated_a)
    rows_mod_b = spread_rows(member, modulated_b)
    mid_stream, kept_a = block_forward(stream_in, rows_mod_a, params_a, spatial_index, pad_mask, 0)
    result, kept_b = block_forward(mid_stream, rows_mod_b, params_b, joint_index, pad_mask, 1)
    grad_top = cotangent.astype(jnp.float32)
    mid_stream, grad_top = lax.optimization_barrier((mid_stream, grad_top))
    kept_b = block_forward(mid_stream, rows_mod_b, params_b, joint_index, pad_mask, 1)[1]
    grad_mid, grad_mod_b, grads_b, table_grad_b = block_backward(
        mid_stream, grad_top, rows_mod_b, params_b, kept_b, joint_index, pad_mask, 1
    )
    grad_ada_b = ada_grad(member, grad_mod_b, cond_act)
    summed_b = sum_block(grads_b, grad_ada_b)
    stream_in, grad_mid = lax.optimization_barrier((stream_in, grad_mid))
    kept_a = block_forward(stream_in, rows_mod_a, params_a, spatial_index, pad_mask, 0)[1]
    grad_stream, grad_mod_a, grads_a, table_grad_a = block_backward(
        stream_in, grad_mid, rows_mod_a, params_a, kept_a, spatial_index, pad_mask, 0
    )
    grad_ada_a = ada_grad(member, grad_mod_a, cond_act)
    summed_a = sum_block(grads_a, grad_ada_a)
    tables = lax.psum((table_grad_a, table_grad_b), "dp")
    return (
        result,
        grad_stream,
        summed_a[0],
        summed_a[1],
        summed_a[2],
        summed_a[3],
        tables[0],
        summed_a[4],
        summed_b[0],
        summed_b[1],
        summed_b[2],
        summed_b[3],
        tables[1],
        summed_b[4],
    )


def solution(mesh):
    in_specs = (
        P(("dp", "mp"), None),
        P("dp", None),
        P("dp", None),
        P(),
        P(),
        P(None, None, "mp"),
        P("mp", None),
        P(None, "mp"),
        P("mp", None),
        P(None, "mp"),
        P(None, "mp"),
        P(None, None, "mp"),
        P("mp", None),
        P(None, "mp"),
        P("mp", None),
        P(None, "mp"),
        P(None, "mp"),
        P(("dp", "mp"), None),
    )
    out_specs = (
        P(("dp", "mp"), None),
        P(("dp", "mp"), None),
        P("dp", None, "mp"),
        P("mp", "dp"),
        P("dp", "mp"),
        P("mp", "dp"),
        P(None, "mp"),
        P("dp", "mp"),
        P("dp", None, "mp"),
        P("mp", "dp"),
        P("dp", "mp"),
        P("mp", "dp"),
        P(None, "mp"),
        P("dp", "mp"),
    )
    return jax.shard_map(local, mesh=mesh, in_specs=in_specs, out_specs=out_specs, check_vma=False)
```

profile of v0, /device:TPU:0, one launch (start us, length us, event | category | flops | bytes accessed | tf_op | source)
XLA Modules:
  0.0 2487.1 jit_solution(14534748873744284094)
XLA Ops:
  33.4 66.7 %while.12 = (s32[]{:T(128)}, f32[16,4096,4]{1,0,2:T(8,128)S(1)}, s32[16,4096]{1,0:T(8,128)S(1)}, bf16[961,4]{0,1:T(4,128)(2,1)S(1)}, s32[]{:T(128)}, /*index=5*/s32[]{:T(128)}) while((s32[]{:T(128)}, f32[16,4096,4]{1,0,2:T(8,128)S(1)}, s32[16,4096]{1,0:T(8,128)S(1)}, bf16[961,4]{0,1:T(4,128)(2,1)S(1)}, s32[]{:T(128)}, ...), condition=%wide.region_3.4_spmd.clone, body=%wide.region_2.3_spmd.clone.sunk | while | flops 35426304 | bytes 384605 | solution.py:62
  121.3 53.0 %reduce-scatter.29.cloned.1.call-done = f32[320,1024]{1,0:T(8,128)} async-done(((f32[1280,1024]{1,0:T(8,128)}), f32[320,1024]{1,0:T(8,128)}) %reduce-scatter.29.cloned.1.call-update) | async-done | bytes 1310736 | tf_op jit(solution)/shard_map/reduce_scatter | solution.py:86
  179.7 25.5 %all-gather.19.cloned.1.call-done = bf16[1280,1024]{1,0:T(8,128)(2,1)} async-done(((bf16[320,1024]{1,0:T(8,128)(2,1)}), bf16[1280,1024]{1,0:T(8,128)(2,1)}) %all-gather.19.cloned.1.call-update) | async-done | bytes 2621456 | tf_op jit(solution)/shard_map/all_gather | solution.py:82
  219.8 48.4 %reduce-scatter.31.cloned.1.call-done = f32[320,1024]{1,0:T(8,128)} async-done(((f32[1280,1024]{1,0:T(8,128)}), f32[320,1024]{1,0:T(8,128)}) %reduce-scatter.31.cloned.1.call-update) | async-done | bytes 1310736 | tf_op jit(solution)/shard_map/reduce_scatter | solution.py:86
  273.6 228.6 %while.13 = (s32[]{:T(128)}, f32[20,5120,4]{1,0,2:T(8,128)}, s32[20,5120]{1,0:T(8,128)}, bf16[2025,4]{0,1:T(4,128)(2,1)S(1)}, s32[]{:T(128)}, /*index=5*/s32[]{:T(128)}) while((s32[]{:T(128)}, f32[20,5120,4]{1,0,2:T(8,128)}, s32[20,5120]{1,0:T(8,128)}, bf16[2025,4]{0,1:T(4,128)(2,1)S(1)}, s32[]{:T(128)}, ...), condition=%wide.region_13.14_spmd.clone, body=%wide.region_12.13_spmd.clone.sunk | while | flops 93312000 | bytes 487325 | solution.py:62
  548.0 51.5 %reduce-scatter.37.cloned.1.call-done = f32[320,1024]{1,0:T(8,128)} async-done(((f32[1280,1024]{1,0:T(8,128)}), f32[320,1024]{1,0:T(8,128)}) %reduce-scatter.37.cloned.1.call-update) | async-done | bytes 1310736 | tf_op jit(solution)/shard_map/reduce_scatter | solution.py:86
  606.6 22.3 all-gather.25.cloned.1.call-done
  675.1 51.5 %reduce-scatter.39.cloned.1.call-done = f32[320,1024]{1,0:T(8,128)} async-done(((f32[1280,1024]{1,0:T(8,128)}), f32[320,1024]{1,0:T(8,128)}) %reduce-scatter.39.cloned.1.call-update) | async-done | bytes 1310736 | tf_op jit(solution)/shard_map/reduce_scatter | solution.py:94
  734.0 25.5 %all-gather.31.cloned.1.call-done = bf16[1280,1024]{1,0:T(8,128)(2,1)} async-done(((bf16[320,1024]{1,0:T(8,128)(2,1)}), bf16[1280,1024]{1,0:T(8,128)(2,1)}) %all-gather.31.cloned.1.call-update) | async-done | bytes 2621456 | tf_op jit(solution)/shard_map/all_gather | solution.py:90
  807.0 51.2 %reduce-scatter.41.cloned.1.call-done = f32[320,1024]{1,0:T(8,128)} async-done(((f32[1280,1024]{1,0:T(8,128)}), f32[320,1024]{1,0:T(8,128)}) %reduce-scatter.41.cloned.1.call-update) | async-done | bytes 1310736 | tf_op jit(solution)/shard_map/reduce_scatter | solution.py:94
  861.8 25.7 %all-gather.21.cloned.1.call-done = bf16[1280,1024]{1,0:T(8,128)(2,1)} async-done(((bf16[320,1024]{1,0:T(8,128)(2,1)}), bf16[1280,1024]{1,0:T(8,128)(2,1)}) %all-gather.21.cloned.1.call-update) | async-done | bytes 2621456 | tf_op jit(solution)/shard_map/all_gather | solution.py:82
  927.3 50.2 %reduce-scatter.33.cloned.1.call-done = f32[320,1024]{1,0:T(8,128)} async-done(((f32[1280,1024]{1,0:T(8,128)}), f32[320,1024]{1,0:T(8,128)}) %reduce-scatter.33.cloned.1.call-update) | async-done | bytes 1310736 | tf_op jit(solution)/shard_map/reduce_scatter | solution.py:86
  988.9 25.3 %all-gather.35.cloned.1.call-done = bf16[1280,1024]{1,0:T(8,128)(2,1)} async-done(((bf16[320,1024]{1,0:T(8,128)(2,1)}), bf16[1280,1024]{1,0:T(8,128)(2,1)}) %all-gather.35.cloned.1.call-update) | async-done | bytes 2621456 | tf_op jit(solution)/shard_map/all_gather | solution.py:82
  1039.3 51.5 %reduce-scatter.43.cloned.1.call-done = f32[320,1024]{1,0:T(8,128)} async-done(((f32[1280,1024]{1,0:T(8,128)}), f32[320,1024]{1,0:T(8,128)}) %reduce-scatter.43.cloned.1.call-update) | async-done | bytes 1310736 | tf_op jit(solution)/shard_map/reduce_scatter | solution.py:86
  1166.0 51.5 %reduce-scatter.45.cloned.1.call-done = f32[320,1024]{1,0:T(8,128)} async-done(((f32[1280,1024]{1,0:T(8,128)}), f32[320,1024]{1,0:T(8,128)}) %reduce-scatter.45.cloned.1.call-update) | async-done | bytes 1310736 | tf_op jit(solution)/shard_map/reduce_scatter | solution.py:94
  1367.7 45.2 %reduce-scatter.57.cloned.1.call-done = f32[320,1024]{1,0:T(8,128)} async-done(((f32[1280,1024]{1,0:T(8,128)}), f32[320,1024]{1,0:T(8,128)}) %reduce-scatter.57.cloned.1.call-update) | async-done | bytes 1310736 | tf_op jit(solution)/shard_map/reduce_scatter | solution.py:86
  1529.4 316.2 %while.15 = (s32[]{:T(128)}, f32[20,2025,4]{1,2,0:T(4,128)}, s32[20,5120]{1,0:T(8,128)}, f32[20,5120,4]{1,0,2:T(8,128)}, s32[]{:T(128)}) while((s32[]{:T(128)}, f32[20,2025,4]{1,2,0:T(4,128)}, s32[20,5120]{1,0:T(8,128)}, f32[20,5120,4]{1,0,2:T(8,128)}, s32[]{:T(128)}) %tuple.133), condition=%wide.region_66.67_spmd.clone, body=%wide.region_65.66_spmd.clone.sunk | while | flops 508032000 | bytes 340049 | solution.py:78
  1852.9 117.5 %while.14 = (s32[]{:T(128)}, f32[16,961,4]{1,2,0:T(4,128)S(1)}, s32[16,4096]{1,0:T(8,128)}, f32[16,4096,4]{1,0,2:T(8,128)}, s32[]{:T(128)}) while((s32[]{:T(128)}, f32[16,961,4]{1,2,0:T(4,128)S(1)}, s32[16,4096]{1,0:T(8,128)}, f32[16,4096,4]{1,0,2:T(8,128)}, s32[]{:T(128)}) %tuple.208), condition=%wide.region_54.55_spmd.clone, body=%wide.region_53.54_spmd.clone.sunk | while | flops 192876544 | bytes 262225 | solution.py:78
  1970.4 39.3 %all-reduce = (f32[961,4]{0,1:T(4,128)}, f32[2025,4]{0,1:T(4,128)}) all-reduce(f32[961,4]{0,1:T(4,128)S(1)} %reduce_sum.401, f32[2025,4]{0,1:T(4,128)S(1)} %reduce_sum.403), channel_id=1, replica_groups=mesh['dp'=8,'mp'=4] {'dp'}, use_global_device_ids=true, to_apply=%region_56.57 | all-reduce | flops 11944 | bytes 95552 | tf_op jit(solution)/shard_map/psum | solution.py:350
  2015.5 76.1 %reduce-scatter.55.cloned.1.call-done = f32[1024,128]{1,0:T(8,128)} async-done(((f32[1024,1024]{1,0:T(8,128)}), f32[1024,128]{1,0:T(8,128)}) %reduce-scatter.55.cloned.1.call-update) | async-done | bytes 524304 | tf_op jit(solution)/shard_map/reduce_scatter | solution.py:133
  2091.7 67.9 %reduce-scatter.51.cloned.1.call-done = f32[256,128]{1,0:T(8,128)} async-done(((f32[256,1024]{1,0:T(8,128)}), f32[256,128]{1,0:T(8,128)}) %reduce-scatter.51.cloned.1.call-update) | async-done | bytes 131088 | tf_op jit(solution)/shard_map/reduce_scatter | solution.py:131
  2159.6 78.3 %reduce-scatter.49.cloned.1.call-done = f32[128,3,256]{2,0,1:T(8,128)} async-done(((f32[1024,3,256]{2,0,1:T(8,128)}), f32[128,3,256]{2,0,1:T(8,128)}) %reduce-scatter.49.cloned.1.call-update) | async-done | bytes 393232 | tf_op jit(solution)/shard_map/reduce_scatter | solution.py:130
  2237.9 121.4 %reduce-scatter.71.cloned.1.call-done = f32[128,1536]{1,0:T(8,128)} async-done(((f32[1024,1536]{1,0:T(8,128)}), f32[128,1536]{1,0:T(8,128)}) %reduce-scatter.71.cloned.1.call-update) | async-done | bytes 786448 | tf_op jit(solution)/shard_map/reduce_scatter | solution.py:134
  2359.3 121.1 %reduce-scatter.59.cloned.1.call-done = f32[128,1536]{1,0:T(8,128)} async-done(((f32[1024,1536]{1,0:T(8,128)}), f32[128,1536]{1,0:T(8,128)}) %reduce-scatter.59.cloned.1.call-update) | async-done | bytes 786448 | tf_op jit(solution)/shard_map/reduce_scatter | solution.py:134
  (733 shorter events, 1387.5 us)
Async XLA Ops:
  32.7 141.6 %reduce-scatter.29.cloned.1.call-start = ((), (), s32[]{:S(2)}) async-start(), calls=%async_computation.25 | async-start | bytes 6553600 | tf_op jit(solution)/shard_map/reduce_scatter | solution.py:86
  216.6 293.8 %all-gather.27.cloned.1.call-start = ((), (), s32[]{:S(2)}) async-start(), calls=%async_computation.33 | async-start | bytes 3276800 | tf_op jit(solution)/shard_map/all_gather | solution.py:82
  273.5 326.0 %reduce-scatter.37.cloned.1.call-start = ((), (), s32[]{:S(2)}) async-start(), calls=%async_computation.34 | async-start | bytes 6553600 | tf_op jit(solution)/shard_map/reduce_scatter | solution.py:86
  606.5 120.1 %reduce-scatter.39.cloned.1.call-start = ((), (), s32[]{:S(2)}) async-start(), calls=%async_computation.36 | async-start | bytes 6553600 | tf_op jit(solution)/shard_map/reduce_scatter | solution.py:94
  733.8 124.5 %reduce-scatter.41.cloned.1.call-start = ((), (), s32[]{:S(2)}) async-start(), calls=%async_computation.38 | async-start | bytes 6553600 | tf_op jit(solution)/shard_map/reduce_scatter | solution.py:94
  861.7 115.8 %reduce-scatter.33.cloned.1.call-start = ((), (), s32[]{:S(2)}) async-start(), calls=%async_computation.29 | async-start | bytes 6553600 | tf_op jit(solution)/shard_map/reduce_scatter | solution.py:86
  988.5 102.3 %reduce-scatter.43.cloned.1.call-start = ((), (), s32[]{:S(2)}) async-start(), calls=%async_computation.41 | async-start | bytes 6553600 | tf_op jit(solution)/shard_map/reduce_scatter | solution.py:86
  1099.7 117.8 %reduce-scatter.45.cloned.1.call-start = ((), (), s32[]{:S(2)}) async-start(), calls=%async_computation.43 | async-start | bytes 6553600 | tf_op jit(solution)/shard_map/reduce_scatter | solution.py:94
  1234.2 124.8 %reduce-scatter.47.cloned.1.call-start = ((), (), s32[]{:S(2)}) async-start(), calls=%async_computation.45 | async-start | bytes 6553600 | tf_op jit(solution)/shard_map/reduce_scatter | solution.py:94
  1300.1 112.8 %reduce-scatter.57.cloned.1.call-start = ((), (), s32[]{:S(2)}) async-start(), calls=%async_computation.50 | async-start | bytes 6553600 | tf_op jit(solution)/shard_map/reduce_scatter | solution.py:86
  1309.1 131.7 %all-gather.23.cloned.1.call-start = ((), (), s32[]{:S(2)}) async-start(), calls=%async_computation.30 | async-start | bytes 3276800 | tf_op jit(solution)/shard_map/all_gather | solution.py:82
  1309.8 206.0 %reduce-scatter.75.cloned.1.call-start = ((), (), s32[]{:S(2)}) async-start(), calls=%async_computation.59 | async-start | bytes 3932160
  1340.0 181.8 %reduce-scatter.73.cloned.1.call-start = ((), (), s32[]{:S(2)}) async-start(), calls=%async_computation.58 | async-start | bytes 3932160
  1433.5 413.3 %reduce-scatter.35.cloned.1.call-start = ((), (), s32[]{:S(2)}) async-start(), calls=%async_computation.31 | async-start | bytes 6553600 | tf_op jit(solution)/shard_map/reduce_scatter | solution.py:86
  1452.4 563.1 %reduce-scatter.65.cloned.1.call-start = ((), (), s32[]{:S(2)}) async-start(), calls=%async_computation.54 | async-start | bytes 4718592 | tf_op jit(solution)/shard_map/reduce_scatter | solution.py:132
  1460.1 555.4 %reduce-scatter.67.cloned.1.call-start = ((), (), s32[]{:S(2)}) async-start(), calls=%async_computation.55 | async-start | bytes 4718592 | tf_op jit(solution)/shard_map/reduce_scatter | solution.py:133
  1469.7 545.8 %reduce-scatter.63.cloned.1.call-start = ((), (), s32[]{:S(2)}) async-start(), calls=%async_computation.53 | async-start | bytes 1179648 | tf_op jit(solution)/shard_map/reduce_scatter | solution.py:131
  1474.4 541.1 %reduce-scatter.61.cloned.1.call-start = ((), (), s32[]{:S(2)}) async-start(), calls=%async_computation.52 | async-start | bytes 3538944 | tf_op jit(solution)/shard_map/reduce_scatter | solution.py:130
  1480.7 534.8 %reduce-scatter.53.cloned.1.call-start = ((), (), s32[]{:S(2)}) async-start(), calls=%async_computation.48 | async-start | bytes 4718592 | tf_op jit(solution)/shard_map/reduce_scatter | solution.py:132
  1488.3 603.4 %reduce-scatter.55.cloned.1.call-start = ((), (), s32[]{:S(2)}) async-start(), calls=%async_computation.49 | async-start | bytes 4718592 | tf_op jit(solution)/shard_map/reduce_scatter | solution.py:133
  1498.0 661.6 %reduce-scatter.51.cloned.1.call-start = ((), (), s32[]{:S(2)}) async-start(), calls=%async_computation.47 | async-start | bytes 1179648 | tf_op jit(solution)/shard_map/reduce_scatter | solution.py:131
  1502.6 735.2 %reduce-scatter.49.cloned.1.call-start = ((), (), s32[]{:S(2)}) async-start(), calls=%async_computation.46 | async-start | bytes 3538944 | tf_op jit(solution)/shard_map/reduce_scatter | solution.py:130
  1509.0 850.3 %reduce-scatter.71.cloned.1.call-start = ((), (), s32[]{:S(2)}) async-start(), calls=%async_computation.57 | async-start | bytes 7077888 | tf_op jit(solution)/shard_map/reduce_scatter | solution.py:134
  1529.3 951.0 %reduce-scatter.59.cloned.1.call-start = ((), (), s32[]{:S(2)}) async-start(), calls=%async_computation.51 | async-start | bytes 7077888 | tf_op jit(solution)/shard_map/reduce_scatter | solution.py:134
  (96 other events, 4025.4 us)
Sparse Core Ops, SparseCore 0:
  121.4 52.8 reduce-scatter.28
  216.7 51.3 reduce-scatter.30
  548.0 51.3 reduce-scatter.36
  675.2 51.3 reduce-scatter.38
  806.8 51.3 reduce-scatter.40
  926.1 51.3 reduce-scatter.32
  1039.4 51.3 reduce-scatter.42
  1166.1 51.3 reduce-scatter.44
  1253.4 51.3 reduce-scatter.68
  1307.5 51.3 reduce-scatter.46
  1361.5 51.3 reduce-scatter.56
  1443.3 37.9 reduce-scatter.74
  1483.8 37.9 reduce-scatter.72
  1524.4 51.3 reduce-scatter.34
  1579.9 87.8 reduce-scatter.64
  1672.4 88.2 reduce-scatter.66
  1764.7 63.5 reduce-scatter.62
  1832.8 74.0 reduce-scatter.60
  1911.5 87.5 reduce-scatter.52
  2003.3 88.2 reduce-scatter.54
  2095.9 63.6 reduce-scatter.50
  2163.8 74.0 reduce-scatter.48
  2242.0 117.1 reduce-scatter.70
  2363.3 117.0 reduce-scatter.58
  (12 shorter events, 307.6 us)
where the time goes:
time: 2500 us; the launch traced here: 2490 us
  waiting for transfers between devices  1150 us (46%)
  matrix products  845 us (34%)
  local copies, waits for them, and re-layouts  306 us (12%)
  other arithmetic  113 us (5%)
  blocking collectives  50.9 us (2%)
    dot_general x36, matrix products, table_one_block(): return jnp.einsum('rn,rh->nh', onehot, grads, precision=HIGHEST)  358 us
    reduce_scatter x8, waiting for transfers between devices, reduce_rows(): return lax.psum_scatter(values, 'mp', scatter_dimension=0, tiled=True)  300 us
    reduce_scatter x2, waiting for transfers between devices, sum_block(): lax.psum_scatter(grad_ada, 'dp', scatter_dimension=0, tiled=True)  242 us
    dot_general x36, matrix products, bias_one_block(): return jnp.dot(onehot, bias_table, preferred_element_type=jnp.float32)  226 us
    reduce_scatter x4, waiting for transfers between devices, reduce_grads(): return lax.psum_scatter(values, 'mp', scatter_dimension=0, tiled=True)  173 us
    all_gather x8, waiting for transfers between devices, gather_rows(): return lax.all_gather(values, 'mp', axis=0, tiled=True)  123 us
    all_gather x4, waiting for transfers between devices, gather_grads(): return lax.all_gather(values, 'mp', axis=0, tiled=True)  84.9 us
    reduce_scatter x2, waiting for transfers between devices, sum_block(): lax.psum_scatter(grads[0], 'dp', scatter_dimension=0, tiled=True)  78.3 us
  transfers between devices with their start and end apart: 36, of which 26 were waited for; matrix products, arithmetic and copies ran while one was open for 39% of the time, Pallas kernels for 0%

commit v1 on v0

v1 whole, which is shorter than its diff:
```python
import functools

import jax
import jax.numpy as jnp
from jax import lax
from jax.experimental import pallas as pl
from jax.experimental.pallas import tpu as pltpu
from jax.sharding import PartitionSpec as P

FRAMES = 5
SIDE = 16
EPSILON = 1e-06
HIGHEST = lax.Precision.HIGHEST
MESH = pl.DeviceIdType.MESH
F32 = jnp.float32
BF16 = jnp.bfloat16
VMEM_LIMIT = 63 << 20
GELU_K = 0.7978845608028654
GELU_C = 0.044715
ANY = pl.BlockSpec(memory_space=pl.ANY)
VM = pl.BlockSpec(memory_space=pltpu.VMEM)


def dma(shape):
    return pltpu.SemaphoreType.DMA(shape)


def places():
    me = lax.axis_index("mp")
    x = lax.div(me, 2)
    core = lax.rem(me, 2)
    return x, core, x * 2 + 1 - core, (1 - x) * 2 + core


def greet(others):
    barrier = pltpu.get_barrier_semaphore()
    for other in others:
        pl.semaphore_signal(barrier, inc=1, device_id={"mp": other}, device_id_type=MESH)
    pl.semaphore_wait(barrier, len(others))


def remote(src, dst, send_sem, recv_sem, other):
    return pltpu.make_async_remote_copy(
        src_ref=src,
        dst_ref=dst,
        send_sem=send_sem,
        recv_sem=recv_sem,
        device_id={"mp": other},
        device_id_type=MESH,
    )


def loop(count, body):
    def step(i, _):
        body(i)
        return 0

    lax.fori_loop(0, count, step, 0)


def rows16(count, body):
    loop(count // 16, lambda i: body(pl.ds(pl.multiple_of(i * 16, 16), 16)))


def cols(count, width, body):
    loop(count // width, lambda j: body(pl.ds(pl.multiple_of(j * width, width), width)))


def norm(values):
    centred = values - jnp.mean(values, axis=-1, keepdims=True)
    inv = lax.rsqrt(jnp.mean(centred * centred, axis=-1, keepdims=True) + EPSILON)
    return centred * inv, inv


def norm_back(normed, inv, grad):
    mean_g = jnp.mean(grad, axis=-1, keepdims=True)
    mean_gn = jnp.mean(grad * normed, axis=-1, keepdims=True)
    return (grad - mean_g - normed * mean_gn) * inv


def dot(a, b):
    return jnp.dot(a, b, preferred_element_type=F32)


def dot_nt(a, b):
    return lax.dot_general(a, b, (((1,), (1,)), ((), ())), preferred_element_type=F32)


def dot_tn(a, b):
    return lax.dot_general(a, b, (((0,), (0,)), ((), ())), preferred_element_type=F32)


def store_a_to_b(dst, frame, value):
    shaped = value.reshape(2, 4, 2, 8, value.shape[-1])
    for qr in range(2):
        for qc in range(2):
            dst[qr * 2 + qc, pl.ds(pl.multiple_of(frame * 4, 4), 4)] = shaped[qr, :, qc]


def store_b_to_a(dst, window, value):
    shaped = value.reshape(FRAMES, 4, 8, value.shape[-1])
    qr, qc = lax.div(window, 2), lax.rem(window, 2)
    for frame in range(FRAMES):
        dst[frame * 2 + qr, :, qc] = shaped[frame]


def store_a_to_a(dst, frame, value):
    shaped = value.reshape(2, 4, 2, 8, value.shape[-1])
    for qr in range(2):
        dst[frame * 2 + qr] = shaped[qr]


def hand_out(groups, out, send_sem, recv_sem, x, core, sibling):
    copies = []
    for i in range(2):
        copies.append(
            remote(
                groups.at[5 * x + 3 - 3 * core + i],
                out.at[1 + 2 * i],
                send_sem.at[i],
                recv_sem.at[i],
                sibling,
            )
        )
        copies[-1].start()
    for i in range(3):
        out[2 * i] = groups[5 * x + 2 * core + i]
    for copy in copies:
        copy.wait()


def forward_kernel(
    windows,
    last,
    stream,
    mod,
    mask,
    bias,
    qkv_hbm,
    proj_hbm,
    fc1_hbm,
    fc2_hbm,
    h1_out,
    qkv_out,
    prob_out,
    att_out,
    ao_out,
    x1_out,
    h2_out,
    act_out,
    dg_out,
    mo_out,
    y_out,
    qkv_w,
    proj_w,
    fc1_w,
    fc2_w,
    h1,
    qkv,
    prob,
    att,
    ao,
    x1,
    h2,
    act,
    dg,
    mo,
    ps1s,
    ps1r,
    xs1s,
    xs1r,
    ps2s,
    ps2r,
    xs2s,
    xs2r,
    part1,
    part2,
    acc,
    groups,
    w_sem,
    out_sem,
    h1_sem,
    h2_sem,
    ps1_sem,
    ps2_sem,
    xs1_sem,
    xs2_sem,
    hand_sem,
):
    width = h1.shape[1]
    half = width // 2
    model = h1.shape[2]
    heads = bias.shape[0]
    inner = proj_w.shape[0]
    head_dim = inner // heads
    x, core, sibling, partner = places()
    own = pl.ds(pl.multiple_of(core * half, 16), half)
    theirs = pl.ds(pl.multiple_of((1 - core) * half, 16), half)

    weights = [
        pltpu.make_async_copy(src, dst, w_sem.at[i])
        for i, (src, dst) in enumerate(
            ((qkv_hbm, qkv_w), (proj_hbm, proj_w), (fc1_hbm, fc1_w), (fc2_hbm, fc2_w))
        )
    ]
    for copy in weights:
        copy.start()
    saves = [
        (h1, h1_out),
        (qkv, qkv_out),
        (prob, prob_out),
        (att, att_out),
        (ao, ao_out),
        (x1, x1_out),
        (h2, h2_out),
        (act, act_out),
        (dg, dg_out),
        (mo, mo_out),
    ]

    def save(which, f):
        src, dst = saves[which]
        return pltpu.make_async_copy(src.at[f], dst.at[f], out_sem.at[which, f])

    def share(buf, sem, f, rows):
        return remote(buf.at[f, own], buf.at[f, rows], sem.at[0, f], sem.at[1, f], sibling)

    def to_sibling(src, dst, sem, f):
        return remote(src.at[f], dst.at[f], sem.at[0, f], sem.at[1, f], sibling)

    def to_partner(src, dst, sem, f):
        return remote(src.at[f], dst.at[f], sem.at[0, f], sem.at[1, f], partner)

    greet((sibling, partner))

    def first_norm(f):
        def some(r):
            normed, _ = norm(stream[f, r].astype(F32))
            h1[f, pl.ds(pl.multiple_of(core * half + r.start, 16), 16)] = (
                normed * (1.0 + mod[1:2]) + mod[0:1]
            ).astype(BF16)

        rows16(half, some)
        share(h1, h1_sem, f, own).start()

    loop(windows, first_norm)
    weights[0].wait()
    weights[1].wait()

    lane_head = lax.div(lax.broadcasted_iota(jnp.int32, (width, inner), 1), head_dim)

    def attention(f):
        share(h1, h1_sem, f, theirs).wait_recv()
        save(0, f).start()
        rows = h1[f]

        def project(c):
            qkv[f, :, c] = dot(rows, qkv_w[:, c]).astype(BF16)

        cols(3 * inner, inner, project)
        save(1, f).start()
        queries = qkv[f, :, :inner] * BF16(head_dim ** (-0.5))
        keys = qkv[f, :, inner : 2 * inner]
        vals = qkv[f, :, 2 * inner :]
        zero = jnp.zeros((), BF16)
        out = jnp.zeros((width, inner), F32)
        for h in range(heads):
            scores = dot_nt(jnp.where(lane_head == h, queries, zero), keys)
            scores = scores + bias[h, :, :width].astype(F32) + mask[f]
            weight = jnp.exp(scores - jnp.max(scores, axis=-1, keepdims=True))
            p = (weight * (1.0 / jnp.sum(weight, axis=-1, keepdims=True))).astype(BF16)
            prob[f, h] = p
            out = out + dot(p, jnp.where(lane_head == h, vals, zero))
        att[f] = out.astype(BF16)
        save(2, f).start()
        save(3, f).start()

        def send_half(c):
            ps1s[f, :, c] = dot(att[f, theirs], proj_w[:, c]).astype(BF16)

        def keep_half(c):
            part1[:, c] = dot(att[f, own], proj_w[:, c])

        cols(model, 512, send_half)
        to_sibling(ps1s, ps1r, ps1_sem, f).start()
        cols(model, 512, keep_half)

    def pair_sum(part, recv, sem, sends, send_to, x_sem, f):
        recv.wait_recv()

        def some(r):
            sends[f, r] = (part[r] + recv_buf(sem)[f, r].astype(F32)).astype(BF16)

        rows16(half, some)
        send_to.start()

    def recv_buf(sem):
        return ps1r if sem is ps1_sem else ps2r

    def sum_first(f):
        pair_sum(
            part1,
            to_sibling(ps1s, ps1r, ps1_sem, f),
            ps1_sem,
            xs1s,
            to_partner(xs1s, xs1r, xs1_sem, f),
            xs1_sem,
            f,
        )

    def sum_second(f):
        pair_sum(
            part2,
            to_sibling(ps2s, ps2r, ps2_sem, f),
            ps2_sem,
            xs2s,
            to_partner(xs2s, xs2r, xs2_sem, f),
            xs2_sem,
            f,
        )

    def middle(f):
        to_partner(xs1s, xs1r, xs1_sem, f).wait_recv()

        def some(r):
            total = xs1s[f, r].astype(F32) + xs1r[f, r].astype(F32)
            mid = stream[f, r].astype(F32) + mod[2:3] * total
            ao[f, r] = total.astype(BF16)
            x1[f, r] = mid
            normed, _ = norm(mid)
            h2[f, pl.ds(pl.multiple_of(core * half + r.start, 16), 16)] = (
                normed * (1.0 + mod[4:5]) + mod[3:4]
            ).astype(BF16)

        rows16(half, some)
        share(h2, h2_sem, f, own).start()
        save(4, f).start()
        save(5, f).start()

    def mlp(f):
        share(h2, h2_sem, f, theirs).wait_recv()
        save(6, f).start()

        def up(c):
            u = dot(h2[f], fc1_w[:, c])
            sq = u * u
            t = jnp.tanh(GELU_K * (u + GELU_C * u * sq))
            one_t = 0.5 * (1.0 + t)
            act[f, :, c] = (u * one_t).astype(BF16)
            slope = one_t + (0.5 * GELU_K) * u * (1.0 - t * t) * (1.0 + (3.0 * GELU_C) * sq)
            dg[f, :, c] = slope.astype(BF16)

        cols(act.shape[2], 256, up)
        save(7, f).start()
        save(8, f).start()

        def send_half(c):
            ps2s[f, :, c] = dot(act[f, theirs], fc2_w[:, c]).astype(BF16)

        def keep_half(c):
            part2[:, c] = dot(act[f, own], fc2_w[:, c])

        cols(model, 256, send_half)
        to_sibling(ps2s, ps2r, ps2_sem, f).start()
        cols(model, 256, keep_half)

    def finish(f):
        to_partner(xs2s, xs2r, xs2_sem, f).wait_recv()

        def some(r):
            total = xs2s[f, r].astype(F32) + xs2r[f, r].astype(F32)
            mo[f, r] = total.astype(BF16)
            acc[r] = x1[f, r] + mod[5:6] * total

        rows16(half, some)
        save(9, f).start()
        if last:
            store_b_to_a(groups, f, acc[...])
        else:
            store_a_to_b(y_out, f, acc[...])

    def step(t):
        @pl.when((t >= 2) & (t < windows + 2))
        def _():
            @pl.when(t == 2)
            def _():
                weights[2].wait()
                weights[3].wait()

            mlp(t - 2)

        @pl.when(t < windows)
        def _():
            attention(t)

        @pl.when((t >= 2) & (t < windows + 2))
        def _():
            sum_second(t - 2)

        @pl.when(t < windows)
        def _():
            sum_first(t)

        @pl.when(t >= 3)
        def _():
            finish(t - 3)

        @pl.when((t >= 1) & (t < windows + 1))
        def _():
            middle(t - 1)

    loop(windows + 3, step)
    if last:
        hand_out(groups, y_out, hand_sem.at[0], hand_sem.at[1], x, core, sibling)

    def drain(f):
        for which in range(len(saves)):
            save(which, f).wait()
        share(h1, h1_sem, f, own).wait_send()
        share(h2, h2_sem, f, own).wait_send()
        to_sibling(ps1s, ps1r, ps1_sem, f).wait_send()
        to_sibling(ps2s, ps2r, ps2_sem, f).wait_send()
        to_partner(xs1s, xs1r, xs1_sem, f).wait_send()
        to_partner(xs2s, xs2r, xs2_sem, f).wait_send()

    loop(windows, drain)


def block_forward(stream, mod, params, bias, mask, last, collective_id):
    qkv_w, proj_w, fc1_w, fc2_w = params
    windows, half, model = stream.shape
    width = 2 * half
    heads = bias.shape[0]
    inner = proj_w.shape[0]
    hidden = fc1_w.shape[1]
    sds = jax.ShapeDtypeStruct
    saved = [
        sds((windows, width, model), BF16),
        sds((windows, width, 3 * inner), BF16),
        sds((windows, heads, width, width), BF16),
        sds((windows, width, inner), BF16),
        sds((windows, half, model), BF16),
        sds((windows, half, model), F32),
        sds((windows, width, model), BF16),
        sds((windows, width, hidden), BF16),
        sds((windows, width, hidden), BF16),
        sds((windows, half, model), BF16),
    ]
    if last:
        y_shape = sds((FRAMES, 4, 2, 8, model), F32)
        groups = (2 * FRAMES, 4, 2, 8, model)
    else:
        y_shape = sds((4, FRAMES * 4, 8, model), F32)
        groups = (1, 1, 1, 8, model)
    own_buf = pltpu.VMEM((windows, half, model), BF16)
    return pl.pallas_call(
        functools.partial(forward_kernel, windows, last),
        out_shape=saved + [y_shape],
        in_specs=[VM] * 4 + [ANY] * 4,
        out_specs=[ANY] * len(saved) + [VM],
        scratch_shapes=[pltpu.VMEM(w.shape, w.dtype) for w in params]
        + [pltpu.VMEM(s.shape, s.dtype) for s in saved]
        + [own_buf] * 8
        + [pltpu.VMEM((half, model), F32)] * 3
        + [
            pltpu.VMEM(groups, F32),
            dma((4,)),
            dma((len(saved), windows)),
        ]
        + [dma((2, windows))] * 6
        + [dma((2, 2))],
        compiler_params=pltpu.CompilerParams(
            collective_id=collective_id, has_side_effects=True, vmem_limit_bytes=VMEM_LIMIT
        ),
        name="forward_last" if last else "forward_first",
    )(stream, mod, mask, bias, qkv_w, proj_w, fc1_w, fc2_w)


def backward_kernel(
    windows,
    last,
    grad_y,
    mod,
    ao,
    mo,
    x1_hbm,
    x_hbm,
    h1_hbm,
    qkv_hbm,
    prob_hbm,
    att_hbm,
    h2_hbm,
    act_hbm,
    dg_hbm,
    qkv_whbm,
    proj_whbm,
    fc1_whbm,
    fc2_whbm,
    gx_out,
    weight_out,
    bias_out,
    mod_out,
    qkv_w,
    proj_w,
    fc1_w,
    fc2_w,
    x1,
    xin,
    h1,
    qkv,
    prob,
    att,
    h2,
    act,
    dg,
    gm,
    ga,
    gh,
    gqkv,
    gatt,
    turned,
    ps1s,
    ps1r,
    xs1s,
    xs1r,
    ps2s,
    ps2r,
    xs2s,
    xs2r,
    part1,
    part2,
    acc,
    groups,
    wgrad,
    wout,
    msum,
    mtot,
    mrecv,
    w_sem,
    in_sem,
    gm_sem,
    ga_sem,
    ps1_sem,
    ps2_sem,
    xs1_sem,
    xs2_sem,
    hand_sem,
    mod_sem,
    wout_sem,
):
    _, half, model = grad_y.shape
    width = 2 * half
    heads = prob.shape[1]
    inner = proj_w.shape[0]
    head_dim = inner // heads
    hidden = fc1_w.shape[1]
    scale = head_dim ** (-0.5)
    x, core, sibling, partner = places()
    own = pl.ds(pl.multiple_of(core * half, 16), half)
    theirs = pl.ds(pl.multiple_of((1 - core) * half, 16), half)

    weights = [
        pltpu.make_async_copy(src, dst, w_sem.at[i])
        for i, (src, dst) in enumerate(
            (
                (fc2_whbm, fc2_w),
                (fc1_whbm, fc1_w),
                (proj_whbm, proj_w),
                (qkv_whbm, qkv_w),
                (x1_hbm, x1),
            )
        )
    ]
    for copy in weights:
        copy.start()

    streams = [
        (act_hbm, act),
        (dg_hbm, dg),
        (h2_hbm, h2),
        (qkv_hbm, qkv),
        (prob_hbm, prob),
        (att_hbm, att),
        (h1_hbm, h1),
        (x_hbm, xin),
    ]

    def fetch(which, f):
        src, dst = streams[which]
        slot = lax.rem(f, 2)
        return pltpu.make_async_copy(src.at[f], dst.at[slot], in_sem.at[which, slot])

    def share(buf, sem, f, rows):
        return remote(buf.at[f, own], buf.at[f, rows], sem.at[0, f], sem.at[1, f], sibling)

    def to_sibling(src, dst, sem, f):
        return remote(src.at[f], dst.at[f], sem.at[0, f], sem.at[1, f], sibling)

    def to_partner(src, dst, sem, f):
        return remote(src.at[f], dst.at[f], sem.at[0, f], sem.at[1, f], partner)

    for which in range(3):
        fetch(which, 0).start()
    greet((sibling, partner))

    def top(f):
        def some(r):
            gm[f, pl.ds(pl.multiple_of(core * half + r.start, 16), 16)] = (
                mod[5:6] * grad_y[f, r]
            ).astype(BF16)

        rows16(half, some)
        share(gm, gm_sem, f, own).start()

    loop(windows, top)
    msum[...] = jnp.zeros_like(msum)
    bias_out[...] = jnp.zeros_like(bias_out)

    def zero_some(r):
        wgrad[r] = jnp.zeros((16, wgrad.shape[1]), F32)

    rows16(model, zero_some)

    lane_head = lax.div(lax.broadcasted_iota(jnp.int32, (width, inner), 1), head_dim)
    zero = jnp.zeros((), BF16)

    def mlp_back(f):
        slot = lax.rem(f, 2)
        for which in range(3):
            fetch(which, f).wait()
        share(gm, gm_sem, f, theirs).wait_recv()

        def up(c):
            back = dot_nt(gm[f], fc2_w[c, :])
            gh[:, c] = (back * dg[slot, :, c].astype(F32)).astype(BF16)

        cols(hidden, 256, up)

        def send_half(c):
            ps1s[f, :, c] = dot_nt(gh[theirs], fc1_w[c, :]).astype(BF16)

        def keep_half(c):
            part1[:, c] = dot_nt(gh[own], fc1_w[c, :])

        cols(model, 256, send_half)
        to_sibling(ps1s, ps1r, ps1_sem, f).start()
        cols(model, 256, keep_half)

    base_fc1 = 4 * inner
    base_fc2 = 4 * inner + hidden

    def add_weight(left, right, base, count):
        turned[...] = left.T

        def some(c):
            where = pl.ds(pl.multiple_of(base + c.start, 256), 256)

            def some_rows(r):
                wgrad[r, where] += dot(turned[r], right[:, c])

            cols(model, 256, some_rows)

        cols(count, 256, some)

    def mlp_weights(f):
        slot = lax.rem(f, 2)
        add_weight(h2[slot], gh, base_fc1, hidden)
        add_weight(gm[f], act.at[slot], base_fc2, hidden)

    def attention_back(f):
        slot = lax.rem(f, 2)
        for which in range(3, 7):
            fetch(which, f).wait()
        share(ga, ga_sem, f, theirs).wait_recv()
        grad_att = dot_nt(ga[f], proj_w[...]).astype(BF16)
        grad_att_t = grad_att.T
        queries_t = qkv[slot, :, :inner].T
        keys = qkv[slot, :, inner : 2 * inner] * BF16(scale)
        vals = qkv[slot, :, 2 * inner :]
        grad_q = jnp.zeros((width, inner), F32)
        grad_k, grad_v = [], []
        for h in range(heads):
            part = slice(h * head_dim, (h + 1) * head_dim)
            p = prob[slot, h]
            grad_p = dot_nt(jnp.where(lane_head == h, grad_att, zero), vals)
            pf = p.astype(F32)
            weighted = pf * grad_p
            grad_s = weighted - pf * jnp.sum(weighted, axis=-1, keepdims=True)
            bias_out[h, :, :width] += grad_s
            rounded = grad_s.astype(BF16)
            grad_q = grad_q + dot(rounded, jnp.where(lane_head == h, keys, zero))
            grad_v.append(dot(grad_att_t[part], p))
            grad_k.append(dot(queries_t[part], rounded) * scale)
        gqkv[:, :inner] = grad_q.astype(BF16)
        gqkv[:, inner : 2 * inner] = jnp.concatenate(grad_k, axis=0).astype(BF16).T
        gqkv[:, 2 * inner :] = jnp.concatenate(grad_v, axis=0).astype(BF16).T

        def send_half(c):
            ps2s[f, :, c] = dot_nt(gqkv[theirs], qkv_w[c, :]).astype(BF16)

        def keep_half(c):
            part2[:, c] = dot_nt(gqkv[own], qkv_w[c, :])

        cols(model, 256, send_half)
        to_sibling(ps2s, ps2r, ps2_sem, f).start()
        cols(model, 256, keep_half)

    def attention_weights(f):
        slot = lax.rem(f, 2)
        add_weight(h1[slot], gqkv, 0, 3 * inner)
        add_weight(ga[f], att.at[slot], 3 * inner, inner)

    def sum_first(f):
        to_sibling(ps1s, ps1r, ps1_sem, f).wait_recv()

        def some(r):
            xs1s[f, r] = (part1[r] + ps1r[f, r].astype(F32)).astype(BF16)

        rows16(half, some)
        to_partner(xs1s, xs1r, xs1_sem, f).start()

    def sum_second(f):
        to_sibling(ps2s, ps2r, ps2_sem, f).wait_recv()

        def some(r):
            xs2s[f, r] = (part2[r] + ps2r[f, r].astype(F32)).astype(BF16)

        rows16(half, some)
        to_partner(xs2s, xs2r, xs2_sem, f).start()

    def fold(values):
        return values.reshape(2, 8, model).sum(axis=0)

    def middle(f):
        to_partner(xs1s, xs1r, xs1_sem, f).wait_recv()

        def some(r):
            grad_h = xs1s[f, r].astype(F32) + xs1r[f, r].astype(F32)
            normed, inv = norm(x1[f, r])
            gy = grad_y[f, r]
            grad_mid = gy + norm_back(normed, inv, grad_h * (1.0 + mod[4:5]))
            msum[2] += fold(grad_mid * ao[f, r].astype(F32))
            msum[3] += fold(grad_h)
            msum[4] += fold(grad_h * normed)
            msum[5] += fold(gy * mo[f, r].astype(F32))
            x1[f, r] = grad_mid
            ga[f, pl.ds(pl.multiple_of(core * half + r.start, 16), 16)] = (
                mod[2:3] * grad_mid
            ).astype(BF16)

        rows16(half, some)
        share(ga, ga_sem, f, own).start()

    def finish(f):
        slot = lax.rem(f, 2)
        fetch(7, f).wait()
        to_partner(xs2s, xs2r, xs2_sem, f).wait_recv()

        def some(r):
            grad_h = xs2s[f, r].astype(F32) + xs2r[f, r].astype(F32)
            normed, inv = norm(xin[slot, r].astype(F32))
            msum[0] += fold(grad_h)
            msum[1] += fold(grad_h * normed)
            acc[r] = x1[f, r] + norm_back(normed, inv, grad_h * (1.0 + mod[1:2]))

        rows16(half, some)
        if last:
            store_b_to_a(gx_out, f, acc[...])
        else:
            store_a_to_a(groups, f, acc[...])

    def step(t):
        @pl.when(t + 1 < windows)
        def _():
            for which in range(3):
                fetch(which, t + 1).start()

        @pl.when((t >= 1) & (t < windows + 1))
        def _():
            for which in range(3, 7):
                fetch(which, t - 1).start()

        @pl.when((t >= 2) & (t < windows + 2))
        def _():
            fetch(7, t - 2).start()

        @pl.when((t >= 2) & (t < windows + 2))
        def _():
            @pl.when(t == 2)
            def _():
                weights[2].wait()
                weights[3].wait()

            attention_back(t - 2)

        @pl.when(t < windows)
        def _():
            @pl.when(t == 0)
            def _():
                weights[0].wait()
                weights[1].wait()

            mlp_back(t)

        @pl.when((t >= 2) & (t < windows + 2))
        def _():
            sum_second(t - 2)

        @pl.when(t < windows)
        def _():
            sum_first(t)

        @pl.when((t >= 2) & (t < windows + 2))
        def _():
            attention_weights(t - 2)

        @pl.when(t < windows)
        def _():
            mlp_weights(t)

        @pl.when(t >= 3)
        def _():
            finish(t - 3)

        @pl.when((t >= 1) & (t < windows + 1))
        def _():
            @pl.when(t == 1)
            def _():
                weights[4].wait()

            middle(t - 1)

    loop(windows + 3, step)

    for i in range(6):
        mtot[i : i + 1] = jnp.sum(msum[i], axis=0, keepdims=True)
    mod_copy = remote(mtot, mrecv, mod_sem.at[0], mod_sem.at[1], sibling)
    mod_copy.start()

    def round_some(i):
        slot = lax.rem(i, 2)
        r = pl.ds(pl.multiple_of(i * 128, 128), 128)
        out = pltpu.make_async_copy(wout.at[slot], weight_out.at[r], wout_sem.at[slot])

        @pl.when(i >= 2)
        def _():
            out.wait()

        wout[slot] = wgrad[r].astype(BF16)
        out.start()

    loop(model // 128, round_some)
    for i in range(model // 128 - 2, model // 128):
        pltpu.make_async_copy(
            wout.at[i % 2], weight_out.at[pl.ds(i * 128, 128)], wout_sem.at[i % 2]
        ).wait()
    mod_copy.wait()
    mod_out[...] = mtot[...] + mrecv[...]
    if not last:
        hand_out(groups, gx_out, hand_sem.at[0], hand_sem.at[1], x, core, sibling)

    def drain(f):
        share(gm, gm_sem, f, own).wait_send()
        share(ga, ga_sem, f, own).wait_send()
        to_sibling(ps1s, ps1r, ps1_sem, f).wait_send()
        to_sibling(ps2s, ps2r, ps2_sem, f).wait_send()
        to_partner(xs1s, xs1r, xs1_sem, f).wait_send()
        to_partner(xs2s, xs2r, xs2_sem, f).wait_send()

    loop(windows, drain)


def block_backward(stream, grad_y, mod, params, kept, padded, last, collective_id):
    qkv_w, proj_w, fc1_w, fc2_w = params
    h1, qkv, prob, att, ao, x1, h2, act, dg, mo = kept
    windows, half, model = stream.shape
    width = 2 * half
    heads = prob.shape[1]
    inner = proj_w.shape[0]
    hidden = fc1_w.shape[1]
    total = 4 * inner + 2 * hidden
    sds = jax.ShapeDtypeStruct
    if last:
        gx_shape = sds((2 * FRAMES, 4, 2, 8, model), F32)
        groups = (1, 1, 1, 8, model)
    else:
        gx_shape = sds((FRAMES, 4, 2, 8, model), F32)
        groups = (2 * FRAMES, 4, 2, 8, model)
    own_buf = pltpu.VMEM((windows, half, model), BF16)
    all_buf = pltpu.VMEM((windows, width, model), BF16)

    def two(array):
        return pltpu.VMEM((2,) + array.shape[1:], array.dtype)

    return pl.pallas_call(
        functools.partial(backward_kernel, windows, last),
        out_shape=[
            gx_shape,
            sds((model, total), BF16),
            sds((heads, width, padded), F32),
            sds((6, model), F32),
        ],
        in_specs=[VM] * 4 + [ANY] * 13,
        out_specs=[VM, ANY, VM, VM],
        scratch_shapes=[pltpu.VMEM(w.shape, w.dtype) for w in params]
        + [pltpu.VMEM(x1.shape, F32)]
        + [two(a) for a in (stream, h1, qkv, prob, att, h2, act, dg)]
        + [
            all_buf,
            all_buf,
            pltpu.VMEM((width, hidden), BF16),
            pltpu.VMEM((width, 3 * inner), BF16),
            pltpu.VMEM((16, 128), BF16),
            pltpu.VMEM((model, width), BF16),
        ]
        + [own_buf] * 8
        + [pltpu.VMEM((half, model), F32)] * 3
        + [
            pltpu.VMEM(groups, F32),
            pltpu.VMEM((model, total), F32),
            pltpu.VMEM((2, 128, total), BF16),
            pltpu.VMEM((6, 8, model), F32),
            pltpu.VMEM((6, model), F32),
            pltpu.VMEM((6, model), F32),
            dma((5,)),
            dma((8, 2)),
        ]
        + [dma((2, windows))] * 6
        + [dma((2, 2)), dma((2,)), dma((2,))],
        compiler_params=pltpu.CompilerParams(
            collective_id=collective_id, has_side_effects=True, vmem_limit_bytes=VMEM_LIMIT
        ),
        name="backward_last" if last else "backward_first",
    )(
        grad_y,
        mod,
        ao,
        mo,
        x1,
        stream,
        h1,
        qkv,
        prob,
        att,
        h2,
        act,
        dg,
        qkv_w,
        proj_w,
        fc1_w,
        fc2_w,
    )


def lookup_kernel(index, table, out):
    heads, groups = table.shape[0], table.shape[1]
    rows, width = index.shape

    def some(r):
        for block in range(width // 128):
            c = pl.ds(block * 128, 128)
            row = index[r, c]
            low = row & 127
            high = row >> 7
            found = [jnp.zeros((16, 128), F32) for _ in range(heads)]
            for g in range(groups):
                here = high == g
                for h in range(heads):
                    spread = jnp.broadcast_to(table[h, pl.ds(g, 1), :], (16, 128))
                    taken = jnp.take_along_axis(spread, low, axis=1, mode="promise_in_bounds")
                    found[h] = jnp.where(here, taken, found[h])
            for h in range(heads):
                out[h, r, c] = found[h].astype(BF16)

    rows16(rows, some)


def bias_lookup(index, table):
    rows, heads = table.shape
    groups = (rows + 127) // 128
    spread = jnp.pad(table.astype(F32), ((0, groups * 128 - rows), (0, 0))).T
    return pl.pallas_call(
        lookup_kernel,
        out_shape=jax.ShapeDtypeStruct((heads,) + index.shape, BF16),
        name="bias_lookup",
    )(index, spread.reshape(heads, groups, 128))


def scatter_kernel(index, grad, out):
    heads = grad.shape[0]
    groups = out.shape[1] // heads
    rows, width = index.shape
    out[...] = jnp.zeros_like(out)
    low_rows = lax.broadcasted_iota(jnp.int32, (128, width), 0)
    high_rows = lax.broadcasted_iota(jnp.int32, (groups, width), 0)

    def some(rb):
        r = pl.ds(pl.multiple_of(rb * 8, 8), 8)
        index_rows = index[r, :]
        low = index_rows & 127
        high = index_rows >> 7
        grads = [grad[h, r, :] for h in range(heads)]
        total = out[...]
        for i in range(8):
            onehot = jnp.where(low_rows == low[i : i + 1], 1.0, 0.0).astype(BF16)
            here = high_rows == high[i : i + 1]
            placed = jnp.concatenate(
                [jnp.where(here, g[i : i + 1], 0.0) for g in grads], axis=0
            ).astype(BF16)
            total = total + dot_nt(onehot, placed)
        out[...] = total

    loop(rows // 8, some)


def table_scatter(index, grad, table_len):
    heads = grad.shape[0]
    groups = (table_len + 127) // 128
    out = pl.pallas_call(
        scatter_kernel,
        out_shape=jax.ShapeDtypeStruct((128, heads * groups), F32),
        name="table_scatter",
    )(index, grad)
    return out.reshape(128, heads, groups)


def reduce_kernel(bits, parts, given, out, *scratch):
    bufs, own, sends, recvs, loads = scratch[:bits], *scratch[bits:]
    me = lax.axis_index("dp")
    mine = [lax.rem(lax.div(me, 1 << b), 2) for b in range(bits)]
    others = [me + (1 - 2 * mine[b]) * (1 << b) for b in range(bits)]
    rows, columns = own.shape[1], own.shape[2]
    share = columns // parts
    fetches = []
    for part in range(parts):
        c = pl.ds(part * share, share)
        fetches.append(pltpu.make_async_copy(given.at[:, :, c], own.at[:, :, c], loads.at[part]))
        fetches[-1].start()
    barrier = pltpu.get_barrier_semaphore()
    for other in others:
        pl.semaphore_signal(barrier, inc=1, device_id={"dp": other}, device_id_type=MESH)
    pl.semaphore_wait(barrier, bits)

    def slice_of(b, j, low):
        index = j * (1 << (b + 1)) + low * (1 << b)
        for lower in range(b):
            index = index + mine[lower] * (1 << lower)
        return index

    def copy(b, j, part):
        c = pl.ds(part * share, share)
        src = own.at[slice_of(b, j, 1 - mine[b]), :, c]
        sem = (b, part, j)
        return pltpu.make_async_remote_copy(
            src_ref=src,
            dst_ref=bufs[b].at[j, :, c],
            send_sem=sends.at[sem],
            recv_sem=recvs.at[sem],
            device_id={"dp": others[b]},
            device_id_type=MESH,
        )

    def add(b, j, part):
        copy(b, j, part).wait_recv()
        c = pl.ds(part * share, share)
        where = slice_of(b, j, mine[b])

        def some(r):
            total = own[where, r, c].astype(F32) + bufs[b][j, r, c].astype(F32)
            if b == bits - 1:
                out[r, c] = total
            else:
                own[where, r, c] = total.astype(BF16)

        rows16(rows, some)

    def first(b, j):
        return 2 * j + (1 - mine[b + 1])

    def second(b, j):
        return 2 * j + mine[b + 1]

    for part in range(parts):
        fetches[part].wait()
        for j in range(1 << (bits - 1)):
            copy(0, j, part).start()
    for part in range(parts):
        for b in range(bits):
            count = 1 << (bits - 1 - b)
            if b == bits - 1:
                add(b, 0, part)
                continue
            for j in range(count // 2):
                add(b, first(b, j), part)
                copy(b + 1, j, part).start()
            for j in range(count // 2):
                add(b, second(b, j), part)
    for part in range(parts):
        for b in range(bits):
            for j in range(1 << (bits - 1 - b)):
                copy(b, j, part).wait_send()


def reduce_weights(grads, size, collective_id):
    rows, columns = grads.shape
    bits = size.bit_length() - 1
    parts = 6
    shaped = grads.reshape(size, rows // size, columns)
    return pl.pallas_call(
        functools.partial(reduce_kernel, bits, parts),
        out_shape=jax.ShapeDtypeStruct((rows // size, columns), F32),
        in_specs=[ANY],
        out_specs=VM,
        scratch_shapes=[
            pltpu.VMEM((1 << (bits - 1 - b), rows // size, columns), BF16) for b in range(bits)
        ]
        + [pltpu.VMEM(shaped.shape, BF16)]
        + [dma((bits, parts, size // 2)), dma((bits, parts, size // 2)), dma((parts,))],
        compiler_params=pltpu.CompilerParams(
            collective_id=collective_id, has_side_effects=True, vmem_limit_bytes=VMEM_LIMIT
        ),
        name="reduce_weights",
    )(shaped)


def place_index(index, layout):
    if layout == 0:
        cut, order, pad = (2, 2, 64), (1, 0, 2), 0
    else:
        cut, order, pad = (FRAMES, 2, 32), (1, 0, 2), 64
    side = index.shape[0]
    both = index.reshape(cut + cut)
    both = both.transpose(order + tuple(3 + o for o in order)).reshape(side, side)
    return jnp.pad(both, ((0, 0), (0, pad)), constant_values=-1)


def local(
    tokens,
    cond,
    pad_mask,
    spatial_index,
    joint_index,
    qkv_a,
    proj_a,
    fc1_a,
    fc2_a,
    table_a,
    ada_a,
    qkv_b,
    proj_b,
    fc1_b,
    fc2_b,
    table_b,
    ada_b,
    cotangent,
    dp_size,
    mp_size,
):
    model = tokens.shape[1]
    inner = proj_a.shape[0]
    hidden = fc1_a.shape[1]
    core = lax.rem(lax.axis_index("mp"), 2)
    params_a = (qkv_a.reshape(model, -1), proj_a, fc1_a, fc2_a)
    params_b = (qkv_b.reshape(model, -1), proj_b, fc1_b, fc2_b)

    def own_rows(values):
        whole = lax.all_gather(values, "mp", axis=0, tiled=True)
        cut = whole.reshape(2 * FRAMES, 2, 4 * SIDE, model)
        return lax.dynamic_index_in_dim(cut, core, axis=1, keepdims=False)

    cond_act = jax.nn.silu(cond.astype(F32)).astype(BF16)
    parts = jnp.concatenate(
        [jnp.dot(cond_act, ada, preferred_element_type=F32) for ada in (ada_a, ada_b)], axis=0
    )
    mods = lax.all_gather(parts, "mp", axis=1, tiled=True).reshape(2, 6, model)

    x_a = own_rows(tokens).reshape(FRAMES, -1, model)
    grad_top = own_rows(cotangent).astype(F32).reshape(FRAMES, 2, 4, 2, 8, model)
    grad_top = grad_top.transpose(1, 3, 0, 2, 4, 5).reshape(4, -1, model)

    index_a = place_index(spatial_index, 0)
    index_b = place_index(joint_index, 1)
    bias_a = bias_lookup(index_a, table_a)
    bias_b = bias_lookup(index_b, table_b)
    hidden_keys = jnp.where(pad_mask.reshape(-1) > 0, 0.0, -1e30).astype(F32)
    mask_a = hidden_keys.reshape(FRAMES, 2, 2, 64).transpose(0, 2, 1, 3).reshape(FRAMES, 1, -1)
    mask_b = hidden_keys.reshape(FRAMES, 2, 2, 4, 2, 8).transpose(1, 4, 2, 0, 3, 5)
    mask_b = mask_b.reshape(4, 1, -1)

    *kept_a, y_a = block_forward(x_a, mods[0], params_a, bias_a, mask_a, False, 1)
    x_b = y_a.reshape(4, -1, model)
    *kept_b, output = block_forward(x_b, mods[1], params_b, bias_b, mask_b, True, 2)
    grad_mid, weights_b, grad_bias_b, mod_b = block_backward(
        x_b, grad_top, mods[1], params_b, kept_b, index_b.shape[1], True, 3
    )
    grad_x, weights_a, grad_bias_a, mod_a = block_backward(
        x_a,
        grad_mid.reshape(FRAMES, -1, model),
        mods[0],
        params_a,
        kept_a,
        index_a.shape[1],
        False,
        4,
    )
    table_grad_a = table_scatter(index_a, grad_bias_a, table_a.shape[0])
    table_grad_b = table_scatter(index_b, grad_bias_b, table_b.shape[0])

    summed = reduce_weights(jnp.concatenate([weights_a, weights_b], axis=1), dp_size, 5)

    wide = ada_a.shape[1]
    first = lax.axis_index("mp") * wide
    mod_columns = [
        lax.dynamic_slice_in_dim(m.reshape(-1), first, wide, axis=0) for m in (mod_a, mod_b)
    ]
    small = jnp.concatenate(
        [cond_act.astype(F32).reshape(-1)]
        + mod_columns
        + [table_grad_a.reshape(-1), table_grad_b.reshape(-1)]
    )
    everyone = lax.all_gather(small, "dp", axis=0, tiled=False)
    cut = [model, model + wide, model + 2 * wide, model + 2 * wide + table_grad_a.size]
    conds, cols_a, cols_b, tables_a, tables_b = jnp.split(everyone, cut, axis=1)
    rows_here = model // dp_size
    my_conds = lax.dynamic_slice_in_dim(conds, lax.axis_index("dp") * rows_here, rows_here, axis=1)

    def outer(columns):
        return jnp.einsum("td,tc->dc", my_conds, columns, precision=HIGHEST)

    def table(parts, like, length):
        summed_table = jnp.sum(parts, axis=0).reshape(like.shape)
        return summed_table.transpose(2, 0, 1).reshape(-1, like.shape[1])[:length]

    def split(piece):
        grad_qkv = piece[:, : 3 * inner].reshape(rows_here, 3, inner)
        grad_proj = piece[:, 3 * inner : 4 * inner].T
        grad_fc1 = piece[:, 4 * inner : 4 * inner + hidden]
        grad_fc2 = piece[:, 4 * inner + hidden :].T
        return grad_qkv, grad_proj, grad_fc1, grad_fc2

    total = 4 * inner + 2 * hidden
    return (
        output.reshape(tokens.shape),
        grad_x.reshape(tokens.shape),
        *split(summed[:, :total]),
        table(tables_a, table_grad_a, table_a.shape[0]),
        outer(cols_a),
        *split(summed[:, total:]),
        table(tables_b, table_grad_b, table_b.shape[0]),
        outer(cols_b),
    )


def solution(mesh):
    in_specs = (
        P(("dp", "mp"), None),
        P("dp", None),
        P("dp", None),
        P(),
        P(),
        P(None, None, "mp"),
        P("mp", None),
        P(None, "mp"),
        P("mp", None),
        P(None, "mp"),
        P(None, "mp"),
        P(None, None, "mp"),
        P("mp", None),
        P(None, "mp"),
        P("mp", None),
        P(None, "mp"),
        P(None, "mp"),
        P(("dp", "mp"), None),
    )
    out_specs = (
        P(("dp", "mp"), None),
        P(("dp", "mp"), None),
        P("dp", None, "mp"),
        P("mp", "dp"),
        P("dp", "mp"),
        P("mp", "dp"),
        P(None, "mp"),
        P("dp", "mp"),
        P("dp", None, "mp"),
        P("mp", "dp"),
        P("dp", "mp"),
        P("mp", "dp"),
        P(None, "mp"),
        P("dp", "mp"),
    )
    body = functools.partial(local, dp_size=mesh.shape["dp"], mp_size=mesh.shape["mp"])
    return jax.shard_map(body, mesh=mesh, in_specs=in_specs, out_specs=out_specs, check_vma=False)
```

time: 2500 us -> 764 us (0.31)
  waiting for transfers between devices: 1150 us -> 12.7 us
  matrix products: 845 us -> 6.37 us
  Pallas kernels: 0 us -> 637 us
  local copies, waits for them, and re-layouts: 306 us -> 41 us
  other arithmetic: 113 us -> 12 us
    reduce_scatter x22 -> x0, waiting for transfers between devices: 938 us -> none  [the longest x8 300 us: reduce_rows(): return lax.psum_scatter(values, 'mp', scatter_dimension=0, tiled=True)]
    dot_general x119 -> x4, matrix products: 820 us -> 6.37 us  [the longest x2 3.39 us: outer(): return jnp.einsum('td,tc->dc', my_conds, columns, precision=HIGHEST)]
    pallas_call x0 -> x9, Pallas kernels: none -> 637 us  [the longest x2 265 us: block_backward(): pl.pallas_call(functools.partial(backward_kernel, windows, last), out_sha...]
    all_gather x12 -> x2, waiting for transfers between devices: 208 us -> 11.3 us  [own_rows(): whole = lax.all_gather(values, 'mp', axis=0, tiled=True)]
    dynamic_slice x108 -> x2, local copies, waits for them, and re-layouts: 93.9 us -> 3.89 us  [own_rows(): return lax.dynamic_index_in_dim(cut, core, axis=1, keepdims=False)]
    reduce_sum x30 -> x2, other arithmetic: 53.3 us -> 0.1 us  [table(): summed_table = jnp.sum(parts, axis=0).reshape(like.shape)]
    dynamic_update_slice x72 -> x0, local copies, waits for them, and re-layouts: 49 us -> none  [bias_lookup(): looked = lax.map(bias_one_block, blocks)]
    another operation x22 -> x2, local copies, waits for them, and re-layouts: 42.6 us -> 1.83 us  [the longest x1 0.92 us: local(): table_grad_a.reshape(-1)]
  transfers between devices with their start and end apart: 36 -> 2, of which waited for: 26 -> 1; matrix products, arithmetic and copies ran while one was open for 39% -> 3% of each run, Pallas kernels for 0% -> 2%
where the time goes in v1:
time: 764 us; the launch traced here: 763 us
  Pallas kernels  637 us (83%)
  local copies, waits for them, and re-layouts  41 us (5%)
  blocking collectives  39.9 us (5%)
  between operations  14.4 us (2%)
  waiting for transfers between devices  12.7 us (2%)
  other arithmetic  12 us (2%)
    pallas_call x2, Pallas kernels, block_backward(): pl.pallas_call(functools.partial(backward_kernel, windows, last), out_sha...  265 us
    pallas_call x2, Pallas kernels, block_forward(): pl.pallas_call(functools.partial(forward_kernel, windows, last), out_shap...  171 us
    pallas_call x1, Pallas kernels, reduce_weights(): pl.pallas_call(functools.partial(reduce_kernel, bits, parts), out_shape=j...  159 us
    all_gather x1, blocking collectives, local(): everyone = lax.all_gather(small, 'dp', axis=0, tiled=False)  33.6 us
    pallas_call x2, Pallas kernels, table_scatter(): pl.pallas_call(scatter_kernel, out_shape=jax.ShapeDtypeStruct((128, heads...  27.9 us
  transfers between devices with their start and end apart: 2, of which 1 were waited for; matrix products, arithmetic and copies ran while one was open for 3% of the time, Pallas kernels for 2%

profile of v1, /device:TPU:0, one launch (start us, length us, event | category | flops | bytes accessed | tf_op | source)
XLA Modules:
  0.0 763.3 jit_solution(5650319408432461485)
XLA Ops:
  9.7 2.5 fusion.5
  12.7 6.3 all_gather.16
  23.7 1.6 copy.113.qkv_hbm.qkv_whbm
  26.7 2.2 reshape.161
  28.9 1.8 copy.144
  32.0 1.7 copy.116
  35.3 4.6 bias_lookup.2.bias
  40.8 10.4 %bias_lookup.3.bias = bf16[4,320,384]{2,1,0:T(8,128)(2,1)} custom-call(s32[320,384]{1,0:T(8,128)} %pad.15.index, f32[4,16,128]{2,1,0:T(8,128)} %bitcast.95), custom_call_target="tpu_custom_call" | custom-call | tf_op jit(solution)/shard_map/bias_lookup/pallas_call | solution.py:982
  51.2 2.5 constant_dynamic-slice_fusion.1
  53.7 11.3 %all-gather.6.cloned.1.call-done = bf16[1280,1024]{1,0:T(8,128)(2,1)} async-done(((bf16[320,1024]{1,0:T(8,128)(2,1)}), bf16[1280,1024]{1,0:T(8,128)(2,1)}) %all-gather.6.cloned.1.call-update) | async-done | bytes 2621456 | tf_op jit(solution)/shard_map/all_gather | solution.py:1167
  66.8 1.6 copy.118
  68.4 84.7 %forward_first.1 = (bf16[5,256,1024]{2,1,0:T(8,128)(2,1)}, bf16[5,256,768]{2,1,0:T(8,128)(2,1)}, bf16[5,4,256,256]{3,2,1,0:T(8,128)(2,1)}, bf16[5,256,256]{2,1,0...) custom-call(bf16[5,128,1024]{2,1,0:T(8,128)(2,1)} %bitcast.75, ...), custom_call_target="tpu_custom_call" | custom-call | tf_op jit(solution)/shard_map/forward_first/pallas_call | solution.py:456
  153.2 85.8 %forward_last.1 = (bf16[4,320,1024]{2,1,0:T(8,128)(2,1)}, bf16[4,320,768]{2,1,0:T(8,128)(2,1)}, bf16[4,4,320,320]{3,2,1,0:T(8,128)(2,1)}, bf16[4,320,256]{2,1,0:...) custom-call(f32[4,160,1024]{2,1,0:T(8,128)} %bitcast.77, ...), custom_call_target="tpu_custom_call" | custom-call | tf_op jit(solution)/shard_map/forward_last/pallas_call | solution.py:456
  239.0 128.8 %backward_last.1 = (f32[10,4,2,8,1024]{4,3,2,1,0:T(8,128)}, bf16[1024,3072]{1,0:T(8,128)(2,1)}, f32[4,320,384]{2,1,0:T(8,128)}, f32[6,1024]{1,0:T(8,128)}) custom-call(f32[4,160,1024]{2,1,0:T(8,128)} %bitcast.79, f32[6,1024]{1,0:T(8,128)} %squeeze.12.mod, bf16[4,160,1024]{2,1,0:T(8,128)(2,1)} %get-tuple-element.46.ao, ...), custom_call_target="tpu_custom_call" | custom-call | tf_op jit(solution)/shard_map/backward_last/pallas_call | solution.py:895
  367.8 135.8 %backward_first.1 = (f32[5,4,2,8,1024]{4,3,2,1,0:T(8,128)}, bf16[1024,3072]{1,0:T(8,128)(2,1)}, f32[4,256,256]{2,1,0:T(8,128)}, f32[6,1024]{1,0:T(8,128)}) custom-call(f32[5,128,1024]{2,1,0:T(8,128)} %bitcast.84, f32[6,1024]{1,0:T(8,128)} %squeeze.11.mod, bf16[5,128,1024]{2,1,0:T(8,128)(2,1)} %get-tuple-element.57.ao, ...), custom_call_target="tpu_custom_call" | custom-call | tf_op jit(solution)/shard_map/backward_first/pallas_call | solution.py:895
  503.6 10.8 %pad_maximum_fusion = bf16[1024,6144]{1,0:T(8,128)(2,1)} fusion(bf16[1024,3072]{1,0:T(8,128)(2,1)} %get-tuple-element.69, bf16[1024,3072]{1,0:T(8,128)(2,1)} %get-tuple-element.68), kind=kLoop, calls=%fused_computation | loop fusion | flops 25165824 | bytes 25165824 | tf_op jit(solution)/shard_map/concatenate | solution.py:1209
  514.4 158.7 %reduce_weights.1 = f32[128,6144]{1,0:T(8,128)} custom-call(bf16[8,128,6144]{2,1,0:T(8,128)(2,1)} %bitcast.74), custom_call_target="tpu_custom_call" | custom-call | tf_op jit(solution)/shard_map/reduce_weights/pallas_call | solution.py:1109
  675.3 2.7 slice_bitcast_fusion
  678.0 10.9 %table_scatter.2 = f32[128,32]{1,0:T(8,128)} custom-call(s32[256,256]{1,0:T(8,128)} %reshape.155.index, f32[4,256,256]{2,1,0:T(8,128)} %get-tuple-element.72.grad), custom_call_target="tpu_custom_call" | custom-call | tf_op jit(solution)/shard_map/table_scatter/pallas_call | solution.py:1019
  689.8 17.0 %table_scatter.3 = f32[128,64]{1,0:T(8,128)} custom-call(s32[320,384]{1,0:T(8,128)} %pad.15.index, f32[4,320,384]{2,1,0:T(8,128)} %get-tuple-element.73.grad), custom_call_target="tpu_custom_call" | custom-call | tf_op jit(solution)/shard_map/table_scatter/pallas_call | solution.py:1019
  707.9 33.6 %all-gather = f32[131072]{0:T(1024)S(1)} all-gather(f32[16384]{0:T(1024)S(1)} %constant_dynamic-update-slice_fusion), channel_id=2, replica_groups=mesh['dp'=8,'mp'=4] {'dp'}, dimensions={0}, use_global_device_ids=true | all-gather | bytes 589824 | tf_op jit(solution)/shard_map/all_gather | solution.py:1221
  741.7 1.7 fusion.2
  743.4 1.7 fusion
  752.8 2.5 copy.158
  (81 shorter events, 27.6 us)
Async XLA Ops:
  7.2 5.0 copy-start.5
  7.2 4.9 copy-start
  7.2 44.0 %all-gather.4.cloned.1.call-start = ((), (), s32[]{:S(2)}) async-start(), calls=%async_computation | async-start | bytes 3276800 | tf_op jit(solution)/shard_map/all_gather | solution.py:1167
  7.9 57.1 %all-gather.6.cloned.1.call-start = ((), (), s32[]{:S(2)}) async-start(), calls=%async_computation.1 | async-start | bytes 3276800 | tf_op jit(solution)/shard_map/all_gather | solution.py:1167
  9.7 10.8 %copy-start.4 = (s32[256,256]{1,0:T(8,128)S(1)}, s32[256,256]{1,0:T(8,128)}, u32[]{:S(2)}) copy-start(s32[256,256]{1,0:T(8,128)} %param.21) | copy-start | bytes 786436
  12.1 10.1 %copy-start.9 = (bf16[961,4]{0,1:T(4,128)(2,1)S(1)}, bf16[961,4]{0,1:T(4,128)(2,1)}, u32[]{:S(2)}) copy-start(bf16[961,4]{0,1:T(4,128)(2,1)} %param.27) | copy-start | bytes 23068
  12.7 10.1 %copy-start.1 = (bf16[1024,3,256]{2,0,1:T(8,128)(2,1)S(1)}, bf16[1024,3,256]{2,0,1:T(8,128)(2,1)}, u32[]{:S(2)}) copy-start(bf16[1024,3,256]{2,0,1:T(8,128)(2,1)} %param.23) | copy-start | bytes 4718596
  23.7 3.0 copy-start.3
  30.6 0.7 copy-start.8
  674.3 3.7 copy-start.7
  674.3 3.7 copy-start.6
  749.2 6.2 copy-start.2
Sparse Core Ops, SparseCore 0:
  9.6 28.2 all-gather.3
  39.4 25.5 all-gather.5

commit v2 on v1

v2 whole, which is shorter than its diff:
```python
import functools

import jax
import jax.numpy as jnp
from jax import lax
from jax.experimental import pallas as pl
from jax.experimental.pallas import tpu as pltpu
from jax.sharding import PartitionSpec as P

FRAMES = 5
SIDE = 16
EPSILON = 1e-06
HIGHEST = lax.Precision.HIGHEST
MESH = pl.DeviceIdType.MESH
F32 = jnp.float32
BF16 = jnp.bfloat16
VMEM_LIMIT = 60 << 20
GELU_K = 0.7978845608028654
GELU_C = 0.044715
ANY = pl.BlockSpec(memory_space=pl.ANY)
VM = pl.BlockSpec(memory_space=pltpu.VMEM)


def dma(shape):
    return pltpu.SemaphoreType.DMA(shape)


def places():
    me = lax.axis_index("mp")
    x = lax.div(me, 2)
    core = lax.rem(me, 2)
    return x, core, x * 2 + 1 - core, (1 - x) * 2 + core


def greet(others):
    barrier = pltpu.get_barrier_semaphore()
    for other in others:
        pl.semaphore_signal(barrier, inc=1, device_id={"mp": other}, device_id_type=MESH)
    pl.semaphore_wait(barrier, len(others))


def remote(src, dst, send_sem, recv_sem, other):
    return pltpu.make_async_remote_copy(
        src_ref=src,
        dst_ref=dst,
        send_sem=send_sem,
        recv_sem=recv_sem,
        device_id={"mp": other},
        device_id_type=MESH,
    )


def loop(count, body):
    def step(i, _):
        body(i)
        return 0

    lax.fori_loop(0, count, step, 0)


def rows16(count, body, step=16):
    loop(count // step, lambda i: body(pl.ds(pl.multiple_of(i * step, step), step)))


def norm(values):
    centred = values - jnp.mean(values, axis=-1, keepdims=True)
    inv = lax.rsqrt(jnp.mean(centred * centred, axis=-1, keepdims=True) + EPSILON)
    return centred * inv, inv


def norm_back(normed, inv, grad):
    mean_g = jnp.mean(grad, axis=-1, keepdims=True)
    mean_gn = jnp.mean(grad * normed, axis=-1, keepdims=True)
    return (grad - mean_g - normed * mean_gn) * inv


def dot(a, b):
    return jnp.dot(a, b, preferred_element_type=F32)


def dot_nt(a, b):
    return lax.dot_general(a, b, (((1,), (1,)), ((), ())), preferred_element_type=F32)


def dot_tn(a, b):
    return lax.dot_general(a, b, (((0,), (0,)), ((), ())), preferred_element_type=F32)


def store_a_to_b(dst, frame, value):
    shaped = value.reshape(2, 4, 2, 8, value.shape[-1])
    for qr in range(2):
        for qc in range(2):
            dst[qr * 2 + qc, pl.ds(pl.multiple_of(frame * 4, 4), 4)] = shaped[qr, :, qc]


def store_b_to_a(dst, window, value):
    shaped = value.reshape(FRAMES, 4, 8, value.shape[-1])
    qr, qc = lax.div(window, 2), lax.rem(window, 2)
    for frame in range(FRAMES):
        dst[frame * 2 + qr, :, qc] = shaped[frame]


def store_a_to_a(dst, frame, value):
    shaped = value.reshape(2, 4, 2, 8, value.shape[-1])
    for qr in range(2):
        dst[frame * 2 + qr] = shaped[qr]


def hand_out(groups, out, send_sem, recv_sem, x, core, sibling):
    copies = []
    for i in range(2):
        copies.append(
            remote(
                groups.at[5 * x + 3 - 3 * core + i],
                out.at[1 + 2 * i],
                send_sem.at[i],
                recv_sem.at[i],
                sibling,
            )
        )
        copies[-1].start()
    for i in range(3):
        out[2 * i] = groups[5 * x + 2 * core + i]
    for copy in copies:
        copy.wait()


def forward_kernel(
    windows,
    last,
    stream,
    mod,
    mask,
    bias,
    qkv_hbm,
    proj_hbm,
    fc1_hbm,
    fc2_hbm,
    h1_out,
    qkv_out,
    prob_out,
    att_out,
    ao_out,
    x1_out,
    h2_out,
    act_out,
    dg_out,
    mo_out,
    y_out,
    qkv_w,
    proj_w,
    fc1_w,
    fc2_w,
    h1,
    qkv,
    prob,
    att,
    ao,
    x1,
    h2,
    act,
    dg,
    mo,
    ps1s,
    ps1r,
    xs1s,
    xs1r,
    ps2s,
    ps2r,
    xs2s,
    xs2r,
    part1,
    part2,
    groups,
    w_sem,
    out_sem,
    h1_sem,
    h2_sem,
    ps1_sem,
    ps2_sem,
    xs1_sem,
    xs2_sem,
    hand_sem,
):
    width = h1.shape[1]
    half = width // 2
    model = h1.shape[2]
    heads = bias.shape[0]
    inner = proj_w.shape[0]
    head_dim = inner // heads
    x, core, sibling, partner = places()
    own = pl.ds(pl.multiple_of(core * half, 16), half)
    theirs = pl.ds(pl.multiple_of((1 - core) * half, 16), half)

    weights = [
        pltpu.make_async_copy(src, dst, w_sem.at[i])
        for i, (src, dst) in enumerate(
            ((qkv_hbm, qkv_w), (proj_hbm, proj_w), (fc1_hbm, fc1_w), (fc2_hbm, fc2_w))
        )
    ]
    for copy in weights:
        copy.start()
    saves = [
        (h1, h1_out),
        (qkv, qkv_out),
        (prob, prob_out),
        (att, att_out),
        (ao, ao_out),
        (x1, x1_out),
        (h2, h2_out),
        (act, act_out),
        (dg, dg_out),
        (mo, mo_out),
    ]

    def save(which, f):
        src, dst = saves[which]
        return pltpu.make_async_copy(src.at[f], dst.at[f], out_sem.at[which, f])

    def share(buf, sem, f, rows):
        return remote(buf.at[f, own], buf.at[f, rows], sem.at[0, f], sem.at[1, f], sibling)

    def to_sibling(src, dst, sem, f):
        return remote(src.at[f], dst.at[f], sem.at[0, f], sem.at[1, f], sibling)

    def to_partner(src, dst, sem, f):
        return remote(src.at[f], dst.at[f], sem.at[0, f], sem.at[1, f], partner)

    greet((sibling, partner))

    def first_norm(f):
        normed, _ = norm(stream[f].astype(F32))
        h1[f, own] = (normed * (1.0 + mod[1:2]) + mod[0:1]).astype(BF16)
        share(h1, h1_sem, f, own).start()

    loop(windows, first_norm)
    weights[0].wait()
    weights[1].wait()

    lane_head = lax.div(lax.broadcasted_iota(jnp.int32, (width, inner), 1), head_dim)

    def attention(f):
        share(h1, h1_sem, f, theirs).wait_recv()
        save(0, f).start()
        qkv[f] = dot(h1[f], qkv_w[...]).astype(BF16)
        save(1, f).start()
        queries = qkv[f, :, :inner] * BF16(head_dim ** (-0.5))
        keys = qkv[f, :, inner : 2 * inner]
        vals = qkv[f, :, 2 * inner :]
        zero = jnp.zeros((), BF16)
        out = jnp.zeros((width, inner), F32)
        for h in range(heads):
            scores = dot_nt(jnp.where(lane_head == h, queries, zero), keys)
            scores = scores + bias[h, :, :width].astype(F32) + mask[f]
            weight = jnp.exp(scores - jnp.max(scores, axis=-1, keepdims=True))
            p = (weight * (1.0 / jnp.sum(weight, axis=-1, keepdims=True))).astype(BF16)
            prob[f, h] = p
            out = out + dot(p, jnp.where(lane_head == h, vals, zero))
        att[f] = out.astype(BF16)
        save(2, f).start()
        save(3, f).start()

        ps1s[f] = dot(att[f, theirs], proj_w[...]).astype(BF16)
        to_sibling(ps1s, ps1r, ps1_sem, f).start()
        part1[...] = dot(att[f, own], proj_w[...])

    def sum_first(f):
        to_sibling(ps1s, ps1r, ps1_sem, f).wait_recv()
        xs1s[f] = (part1[...] + ps1r[f].astype(F32)).astype(BF16)
        to_partner(xs1s, xs1r, xs1_sem, f).start()

    def sum_second(f):
        to_sibling(ps2s, ps2r, ps2_sem, f).wait_recv()
        xs2s[f] = (part2[...] + ps2r[f].astype(F32)).astype(BF16)
        to_partner(xs2s, xs2r, xs2_sem, f).start()

    def middle(f):
        to_partner(xs1s, xs1r, xs1_sem, f).wait_recv()

        total = xs1s[f].astype(F32) + xs1r[f].astype(F32)
        mid = stream[f].astype(F32) + mod[2:3] * total
        ao[f] = total.astype(BF16)
        x1[f] = mid
        normed, _ = norm(mid)
        h2[f, own] = (normed * (1.0 + mod[4:5]) + mod[3:4]).astype(BF16)
        share(h2, h2_sem, f, own).start()
        save(4, f).start()
        save(5, f).start()

    def mlp(f):
        share(h2, h2_sem, f, theirs).wait_recv()
        save(6, f).start()

        for start in range(0, act.shape[2], 256):
            c = pl.ds(start, 256)
            u = dot(h2[f], fc1_w[:, c])
            sq = u * u
            t = jnp.tanh(GELU_K * (u + GELU_C * u * sq))
            one_t = 0.5 * (1.0 + t)
            act[f, :, c] = (u * one_t).astype(BF16)
            slope = one_t + (0.5 * GELU_K) * u * (1.0 - t * t) * (1.0 + (3.0 * GELU_C) * sq)
            dg[f, :, c] = slope.astype(BF16)
        save(7, f).start()
        save(8, f).start()
        ps2s[f] = dot(act[f, theirs], fc2_w[...]).astype(BF16)
        to_sibling(ps2s, ps2r, ps2_sem, f).start()
        part2[...] = dot(act[f, own], fc2_w[...])

    def finish(f):
        to_partner(xs2s, xs2r, xs2_sem, f).wait_recv()

        total = xs2s[f].astype(F32) + xs2r[f].astype(F32)
        mo[f] = total.astype(BF16)
        save(9, f).start()
        result = x1[f] + mod[5:6] * total
        if last:
            store_b_to_a(groups, f, result)
        else:
            store_a_to_b(y_out, f, result)

    def step(t):
        @pl.when((t >= 2) & (t < windows + 2))
        def _():
            @pl.when(t == 2)
            def _():
                weights[2].wait()
                weights[3].wait()

            mlp(t - 2)

        @pl.when(t < windows)
        def _():
            attention(t)

        @pl.when((t >= 2) & (t < windows + 2))
        def _():
            sum_second(t - 2)

        @pl.when(t < windows)
        def _():
            sum_first(t)

        @pl.when(t >= 3)
        def _():
            finish(t - 3)

        @pl.when((t >= 1) & (t < windows + 1))
        def _():
            middle(t - 1)

    loop(windows + 3, step)
    if last:
        hand_out(groups, y_out, hand_sem.at[0], hand_sem.at[1], x, core, sibling)

    def drain(f):
        for which in range(len(saves)):
            save(which, f).wait()
        share(h1, h1_sem, f, own).wait_send()
        share(h2, h2_sem, f, own).wait_send()
        to_sibling(ps1s, ps1r, ps1_sem, f).wait_send()
        to_sibling(ps2s, ps2r, ps2_sem, f).wait_send()
        to_partner(xs1s, xs1r, xs1_sem, f).wait_send()
        to_partner(xs2s, xs2r, xs2_sem, f).wait_send()

    loop(windows, drain)


def block_forward(stream, mod, params, bias, mask, last, collective_id):
    qkv_w, proj_w, fc1_w, fc2_w = params
    windows, half, model = stream.shape
    width = 2 * half
    heads = bias.shape[0]
    inner = proj_w.shape[0]
    hidden = fc1_w.shape[1]
    sds = jax.ShapeDtypeStruct
    saved = [
        sds((windows, width, model), BF16),
        sds((windows, width, 3 * inner), BF16),
        sds((windows, heads, width, width), BF16),
        sds((windows, width, inner), BF16),
        sds((windows, half, model), BF16),
        sds((windows, half, model), F32),
        sds((windows, width, model), BF16),
        sds((windows, width, hidden), BF16),
        sds((windows, width, hidden), BF16),
        sds((windows, half, model), BF16),
    ]
    if last:
        y_shape = sds((FRAMES, 4, 2, 8, model), F32)
        groups = (2 * FRAMES, 4, 2, 8, model)
    else:
        y_shape = sds((4, FRAMES * 4, 8, model), F32)
        groups = (1, 1, 1, 8, model)
    own_buf = pltpu.VMEM((windows, half, model), BF16)
    return pl.pallas_call(
        functools.partial(forward_kernel, windows, last),
        out_shape=saved + [y_shape],
        in_specs=[VM] * 4 + [ANY] * 4,
        out_specs=[ANY] * len(saved) + [VM],
        scratch_shapes=[pltpu.VMEM(w.shape, w.dtype) for w in params]
        + [pltpu.VMEM(s.shape, s.dtype) for s in saved]
        + [own_buf] * 8
        + [pltpu.VMEM((half, model), F32)] * 2
        + [
            pltpu.VMEM(groups, F32),
            dma((4,)),
            dma((len(saved), windows)),
        ]
        + [dma((2, windows))] * 6
        + [dma((2, 2))],
        compiler_params=pltpu.CompilerParams(
            collective_id=collective_id, has_side_effects=True, vmem_limit_bytes=VMEM_LIMIT
        ),
        name="forward_last" if last else "forward_first",
    )(stream, mod, mask, bias, qkv_w, proj_w, fc1_w, fc2_w)


def backward_kernel(windows, last, size, names, *refs):
    r = dict(zip(names, refs, strict=True))
    mod, index = r["mod"], r["index"]
    grad, part1, part2, gh, gqkv = r["grad"], r["part1"], r["part2"], r["gh"], r["gqkv"]
    fc1_w, fc2_w, qkv_w, proj_w = r["fc1_w"], r["fc2_w"], r["qkv_w"], r["proj_w"]
    gm, ga, rest, wgrad, gbias = r["gm"], r["ga"], r["rest"], r["wgrad"], r["gbias"]
    ps1s, ps1r, ps2s, ps2r = r["ps1s"], r["ps1r"], r["ps2s"], r["ps2r"]
    xs1s, xs1r, xs2s, xs2r = r["xs1s"], r["xs1r"], r["xs2s"], r["xs2r"]
    buf1, buf2, msum, mtot, mrecv = r["buf1"], r["buf2"], r["msum"], r["mtot"], r["mrecv"]
    _, half, model = grad.shape
    width = 2 * half
    heads = gbias.shape[0]
    inner = proj_w.shape[0]
    head_dim = inner // heads
    hidden = wgrad.shape[1] // 2
    scale = head_dim ** (-0.5)
    chunk = buf1.shape[-1]
    fc_chunks = hidden // chunk
    rest_chunks = 4 * inner // chunk
    x, core, sibling, partner = places()
    own = pl.ds(pl.multiple_of(core * half, 16), half)
    theirs = pl.ds(pl.multiple_of((1 - core) * half, 16), half)
    lines = size // 2
    here = lax.axis_index("dp")
    line, side = lax.div(here, 2), lax.rem(here, 2)

    loads = [
        pltpu.make_async_copy(r[src], r[dst], r["w_sem"].at[i])
        for i, (src, dst) in enumerate(
            (("fc2", "fc2_w"), ("fc1", "fc1_w"), ("proj", "proj_w"), ("qkv", "qkv_w"))
            + (("grad_y", "grad"),)
            + (() if last else (("carry", "rest"),))
        )
    ]
    streams = [
        (r[name], r[name + "_v"])
        for name in ("act", "dg", "h2", "qkv_s", "prob", "att", "h1", "x1", "ao", "mo", "stream")
    ]

    def fetch(which, f):
        src, dst = streams[which]
        slot = lax.rem(f, 2)
        return pltpu.make_async_copy(src.at[f], dst.at[slot], r["in_sem"].at[which, slot])

    def share(buf, sem, f, rows):
        return remote(buf.at[f, own], buf.at[f, rows], sem.at[0, f], sem.at[1, f], sibling)

    def to_sibling(src, dst, sem, f):
        slot = lax.rem(f, 2)
        return remote(src.at[slot], dst.at[slot], sem.at[0, slot], sem.at[1, slot], sibling)

    def first_ps(f):
        return to_sibling(ps1s, ps1r, r["ps1_sem"], f)

    def second_ps(f):
        return to_sibling(ps2s, ps2r, r["ps2_sem"], f)

    def first_xs(f):
        sem = r["xs1_sem"]
        return remote(xs1s.at[f], xs1r.at[f], sem.at[0, f], sem.at[1, f], partner)

    def second_xs(f):
        sem, slot = r["xs2_sem"], lax.rem(f, 2)
        return remote(xs2s.at[slot], xs2r.at[f], sem.at[0, slot], sem.at[1, f], partner)

    def along_dp(src, dst, send_sem, recv_sem, other):
        return pltpu.make_async_remote_copy(
            src_ref=src,
            dst_ref=dst,
            send_sem=send_sem,
            recv_sem=recv_sem,
            device_id={"dp": other},
            device_id_type=MESH,
        )

    def chunk_cols(i):
        return pl.ds(pl.multiple_of(i * chunk, chunk), chunk)

    def across(g, k, i):
        return along_dp(
            g.at[:, 1 - side, :, chunk_cols(i)],
            buf1.at[k, i],
            r["across_sem"].at[0, k, i],
            r["across_sem"].at[1, k, i],
            line * 2 + 1 - side,
        )

    def along(k, i, j):
        to = lax.rem(line + 1 + j, lines)
        return along_dp(
            buf1.at[k, i, to],
            buf2.at[k, i, j],
            r["along_sem"].at[0, k, i, j],
            r["along_sem"].at[1, k, i, j],
            to * 2 + side,
        )

    def reduce_side(g, k, i):
        across(g, k, i).wait_recv()
        both = g[:, side, :, chunk_cols(i)].astype(F32) + buf1[k, i].astype(F32)
        buf1[k, i] = both.astype(BF16)
        loop(lines - 1, lambda j: along(k, i, j).start())

    def reduce_line(k, i):
        loop(lines - 1, lambda j: along(k, i, j).wait_recv())
        return buf1[k, i, line].astype(F32) + jnp.sum(buf2[k, i].astype(F32), axis=0)

    loads[4].start()
    for which in range(3):
        fetch(which, 0).start()
    for copy in loads[:4] + loads[5:]:
        copy.start()

    barrier = pltpu.get_barrier_semaphore()
    for other in (sibling, partner):
        pl.semaphore_signal(barrier, inc=1, device_id={"mp": other}, device_id_type=MESH)
    pl.semaphore_signal(
        barrier, inc=1, device_id={"dp": line * 2 + 1 - side}, device_id_type=MESH
    )
    for j in range(lines - 1):
        pl.semaphore_signal(
            barrier,
            inc=1,
            device_id={"dp": lax.rem(line + 1 + j, lines) * 2 + side},
            device_id_type=MESH,
        )
    pl.semaphore_wait(barrier, 2 + lines)

    loads[4].wait()

    def top(f):
        gm[f, own] = (mod[5:6] * grad[f]).astype(BF16)
        share(gm, r["gm_sem"], f, own).start()

    loop(windows, top)
    if not last:
        loads[5].wait()
        loop(rest_chunks, lambda i: across(rest, 2, i).start())
    msum[...] = jnp.zeros_like(msum)
    gbias[...] = jnp.zeros_like(gbias)
    wgrad[...] = jnp.zeros_like(wgrad)

    lane_head = lax.div(lax.broadcasted_iota(jnp.int32, (width, inner), 1), head_dim)
    zero = jnp.zeros((), BF16)

    def flat(weight):
        value = weight[...]
        return value.reshape(-1, value.shape[-1])

    def mlp_back(f):
        slot = lax.rem(f, 2)
        for which in range(3):
            fetch(which, f).wait()
        share(gm, r["gm_sem"], f, theirs).wait_recv()
        gh[...] = (dot_nt(gm[f], flat(fc2_w)) * r["dg_v"][slot].astype(F32)).astype(BF16)

        @pl.when(f >= 2)
        def _():
            first_ps(f - 2).wait_send()

        ps1s[slot] = dot_nt(gh[theirs], flat(fc1_w)).astype(BF16)
        first_ps(f).start()
        part1[...] = dot_nt(gh[own], flat(fc1_w))

    def sum_first(f):
        slot = lax.rem(f, 2)
        first_ps(f).wait_recv()
        xs1s[f] = (part1[...] + ps1r[slot].astype(F32)).astype(BF16)
        first_xs(f).start()

    def mlp_weights(f):
        slot = lax.rem(f, 2)
        for start in range(0, hidden, 512):
            c = pl.ds(start, 512)
            wgrad[:, c] += dot_tn(r["h2_v"][slot], gh[:, c])
        for start in range(0, hidden, 512):
            c, to = pl.ds(start, 512), pl.ds(hidden + start, 512)
            wgrad[:, to] += dot_tn(gm[f], r["act_v"][slot, :, c])

    def fold(values):
        return values.reshape(half // 8, 8, model).sum(axis=0)

    def middle(f):
        slot = lax.rem(f, 2)
        for which in range(7, 10):
            fetch(which, f).wait()
        first_xs(f).wait_recv()
        grad_h = xs1s[f].astype(F32) + xs1r[f].astype(F32)
        normed, inv = norm(r["x1_v"][slot])
        gy = grad[f]
        grad_mid = gy + norm_back(normed, inv, grad_h * (1.0 + mod[4:5]))
        msum[2] += fold(grad_mid * r["ao_v"][slot].astype(F32))
        msum[3] += fold(grad_h)
        msum[4] += fold(grad_h * normed)
        msum[5] += fold(gy * r["mo_v"][slot].astype(F32))
        grad[f] = grad_mid
        ga[f, own] = (mod[2:3] * grad_mid).astype(BF16)
        share(ga, r["ga_sem"], f, own).start()

    def attention_back(f):
        slot = lax.rem(f, 2)
        qkv = r["qkv_s_v"]
        for which in range(3, 7):
            fetch(which, f).wait()
        share(ga, r["ga_sem"], f, theirs).wait_recv()
        grad_att = dot_nt(ga[f], proj_w[...]).astype(BF16)
        grad_att_t = grad_att.T
        queries_t = qkv[slot, :, :inner].T
        keys = qkv[slot, :, inner : 2 * inner] * BF16(scale)
        vals = qkv[slot, :, 2 * inner :]
        grad_q = jnp.zeros((width, inner), F32)
        grad_k, grad_v = [], []
        for h in range(heads):
            part = slice(h * head_dim, (h + 1) * head_dim)
            p = r["prob_v"][slot, h]
            grad_p = dot_nt(jnp.where(lane_head == h, grad_att, zero), vals)
            pf = p.astype(F32)
            weighted = pf * grad_p
            grad_s = weighted - pf * jnp.sum(weighted, axis=-1, keepdims=True)
            gbias[h, :, :width] += grad_s
            rounded = grad_s.astype(BF16)
            grad_q = grad_q + dot(rounded, jnp.where(lane_head == h, keys, zero))
            grad_v.append(dot(grad_att_t[part], p))
            grad_k.append(dot(queries_t[part], rounded) * scale)
        gqkv[:, :inner] = grad_q.astype(BF16)
        gqkv[:, inner : 2 * inner] = jnp.concatenate(grad_k, axis=0).astype(BF16).T
        gqkv[:, 2 * inner :] = jnp.concatenate(grad_v, axis=0).astype(BF16).T

        @pl.when(f >= 2)
        def _():
            second_ps(f - 2).wait_send()

        ps2s[slot] = dot_nt(gqkv[theirs], qkv_w[...]).astype(BF16)
        second_ps(f).start()
        part2[...] = dot_nt(gqkv[own], qkv_w[...])

    def sum_second(f):
        slot = lax.rem(f, 2)
        second_ps(f).wait_recv()

        @pl.when(f >= 2)
        def _():
            second_xs(f - 2).wait_send()

        xs2s[slot] = (part2[...] + ps2r[slot].astype(F32)).astype(BF16)
        second_xs(f).start()

    def attention_weights(f):
        slot = lax.rem(f, 2)
        for start in range(0, 3 * inner, 384):
            c = pl.ds(start, 384)
            wgrad[:, c] += dot_tn(r["h1_v"][slot], gqkv[:, c])
        wgrad[:, 3 * inner : 4 * inner] += dot_tn(ga[f], r["att_v"][slot])

    def finish(f):
        slot = lax.rem(f, 2)
        fetch(10, f).wait()
        second_xs(f).wait_recv()
        grad_h = xs2s[slot].astype(F32) + xs2r[f].astype(F32)
        normed, inv = norm(r["stream_v"][slot].astype(F32))
        msum[0] += fold(grad_h)
        msum[1] += fold(grad_h * normed)
        grad_x = grad[f] + norm_back(normed, inv, grad_h * (1.0 + mod[1:2]))
        if last:
            store_b_to_a(r["gx"], f, grad_x)
        else:
            grad[f] = grad_x

    def first_step(f):
        @pl.when(f + 1 < windows)
        def _():
            for which in range(3):
                fetch(which, f + 1).start()

        @pl.when(f == 0)
        def _():
            loads[0].wait()
            loads[1].wait()

        mlp_back(f)
        sum_first(f)
        mlp_weights(f)
        if not last:

            @pl.when((f >= 1) & (f <= rest_chunks))
            def _():
                reduce_side(rest, 2, f - 1)

    loop(windows, first_step)

    for which in range(3, 11):
        fetch(which, 0).start()
    shape = fc1_w.shape
    fc1_w[...] = wgrad[:, :hidden].astype(BF16).reshape(shape)
    loop(fc_chunks, lambda i: across(fc1_w, 0, i).start())
    fc2_w[...] = wgrad[:, hidden:].astype(BF16).reshape(shape)
    loop(fc_chunks, lambda i: across(fc2_w, 1, i).start())
    wgrad[:, : 4 * inner] = jnp.zeros((model, 4 * inner), F32)
    for which in range(7, 10):
        fetch(which, 1).start()
    middle(0)
    loads[2].wait()
    loads[3].wait()
    offset = windows - fc_chunks

    def second_step(f):
        @pl.when(f + 1 < windows)
        def _():
            for which in range(3, 7):
                fetch(which, f + 1).start()
            middle(f + 1)

        @pl.when(f + 2 < windows)
        def _():
            for which in range(7, 10):
                fetch(which, f + 2).start()

        attention_back(f)
        sum_second(f)
        attention_weights(f)

        @pl.when(f >= 1)
        def _():
            finish(f - 1)

        @pl.when((f >= 1) & (f + 1 < windows))
        def _():
            fetch(10, f + 1).start()

        @pl.when(f == 0)
        def _():
            fetch(10, 1).start()

        @pl.when(f >= offset)
        def _():
            reduce_side(fc1_w, 0, f - offset)
            reduce_side(fc2_w, 1, f - offset)

    loop(windows, second_step)

    if not last:
        loop(rest_chunks, lambda i: across(rest, 2, i).wait_send())
    rest[...] = wgrad[:, : 4 * inner].astype(BF16).reshape(rest.shape)
    if last:
        carry = pltpu.make_async_copy(rest, r["carry"], r["w_sem"].at[5])
        carry.start()
    else:
        loop(rest_chunks, lambda i: across(rest, 3, i).start())
    finish(windows - 1)
    for i in range(6):
        mtot[i : i + 1] = jnp.sum(msum[i], axis=0, keepdims=True)
    mod_copy = remote(mtot, mrecv, r["mod_sem"].at[0], r["mod_sem"].at[1], sibling)
    mod_copy.start()
    hands = []
    if not last:
        gx = r["gx"]

        def group(j):
            which = 5 * x + j
            rows = pl.ds(pl.multiple_of(lax.rem(which, 2) * 64, 64), 64)
            return lax.div(which, 2), rows

        for i in range(2):
            f, rows = group(3 - 3 * core + i)
            hands.append(
                remote(
                    grad.at[f, rows],
                    gx.at[1 + 2 * i],
                    r["hand_sem"].at[0, i],
                    r["hand_sem"].at[1, i],
                    sibling,
                )
            )
            hands[-1].start()
        for i in range(3):
            f, rows = group(2 * core + i)
            gx[2 * i] = grad[f, rows]

    scatter(index, gbias, r["table"])
    fc_out = r["fc_out"]

    def finish_fc(i):
        for k in range(2):
            fc_out[k, :, chunk_cols(i)] = reduce_line(k, i)

    loop(fc_chunks, finish_fc)
    if not last:

        def finish_carry(i):
            r["carry_out"][:, chunk_cols(i)] = reduce_line(2, i)

        loop(rest_chunks, finish_carry)
        loop(rest_chunks, lambda i: reduce_side(rest, 3, i))

        def finish_rest(i):
            r["rest_out"][:, chunk_cols(i)] = reduce_line(3, i)

        loop(rest_chunks, finish_rest)
    else:
        carry.wait()
    mod_copy.wait()
    r["mod_out"][...] = mtot[...] + mrecv[...]
    for copy in hands:
        copy.wait()

    def drain(f):
        share(gm, r["gm_sem"], f, own).wait_send()
        share(ga, r["ga_sem"], f, own).wait_send()
        first_xs(f).wait_send()

    loop(windows, drain)
    for f in range(windows - 2, windows):
        for copy in (first_ps(f), second_ps(f), second_xs(f)):
            copy.wait_send()

    def drain_chunk(k, g, i):
        across(g, k, i).wait_send()
        loop(lines - 1, lambda j: along(k, i, j).wait_send())

    loop(fc_chunks, lambda i: drain_chunk(0, fc1_w, i))
    loop(fc_chunks, lambda i: drain_chunk(1, fc2_w, i))
    if not last:
        loop(rest_chunks, lambda i: loop(lines - 1, lambda j: along(2, i, j).wait_send()))
        loop(rest_chunks, lambda i: drain_chunk(3, rest, i))


def block_backward(stream, grad_y, mod, params, kept, index, table_len, carry, size, collective_id):
    last = carry is None
    qkv_w, proj_w, fc1_w, fc2_w = params
    h1, qkv, prob, att, ao, x1, h2, act, dg, mo = kept
    windows, half, model = stream.shape
    width = 2 * half
    heads = prob.shape[1]
    inner = proj_w.shape[0]
    hidden = fc1_w.shape[1]
    rows = model // size
    lines = size // 2
    chunk = 256
    chunks = max(hidden, 4 * inner) // chunk
    kinds = 2 if last else 4
    groups = (table_len + 127) // 128
    sds = jax.ShapeDtypeStruct
    sliced = (lines, 2, rows)
    cut = (*sliced, hidden)

    ins, outs, scratch = {}, {}, {}
    ins["grad_y"] = (grad_y, ANY)
    ins["mod"] = (mod, VM)
    ins["index"] = (index, VM)
    for name, value in (
        ("act", act),
        ("dg", dg),
        ("h2", h2),
        ("qkv_s", qkv),
        ("prob", prob),
        ("att", att),
        ("h1", h1),
        ("x1", x1),
        ("ao", ao),
        ("mo", mo),
        ("stream", stream),
    ):
        ins[name] = (value, ANY)
        scratch[name + "_v"] = pltpu.VMEM((2,) + value.shape[1:], value.dtype)
    ins["qkv"] = (qkv_w, ANY)
    ins["proj"] = (proj_w, ANY)
    ins["fc1"] = (fc1_w.reshape(cut), ANY)
    ins["fc2"] = (fc2_w.reshape(cut), ANY)
    if not last:
        ins["carry"] = (carry, ANY)
    if last:
        outs["gx"] = (sds((2 * FRAMES, 4, 2, 8, model), F32), VM)
        outs["carry"] = (sds((*sliced, 4 * inner), BF16), ANY)
    else:
        outs["gx"] = (sds((FRAMES, 4 * SIDE, model), F32), VM)
        outs["carry_out"] = (sds((rows, 4 * inner), F32), VM)
        outs["rest_out"] = (sds((rows, 4 * inner), F32), VM)
    outs["fc_out"] = (sds((2, rows, hidden), F32), VM)
    outs["table"] = (sds((128, heads * groups), F32), VM)
    outs["mod_out"] = (sds((6, model), F32), VM)

    own_all = pltpu.VMEM((windows, half, model), BF16)
    own_two = pltpu.VMEM((2, half, model), BF16)
    own_one = pltpu.VMEM((half, model), F32)
    every = pltpu.VMEM((windows, width, model), BF16)
    scratch.update(
        grad=pltpu.VMEM((windows, half, model), F32),
        part1=own_one,
        part2=own_one,
        gh=pltpu.VMEM((width, hidden), BF16),
        gqkv=pltpu.VMEM((width, 3 * inner), BF16),
        fc1_w=pltpu.VMEM(cut, BF16),
        fc2_w=pltpu.VMEM(cut, BF16),
        qkv_w=pltpu.VMEM(qkv_w.shape, BF16),
        proj_w=pltpu.VMEM(proj_w.shape, BF16),
        gm=every,
        ga=every,
        rest=pltpu.VMEM((*sliced, 4 * inner), BF16),
        wgrad=pltpu.VMEM((model, 2 * hidden), F32),
        gbias=pltpu.VMEM((heads, *index.shape), F32),
        ps1s=own_two,
        ps1r=own_two,
        ps2s=own_two,
        ps2r=own_two,
        xs1s=own_all,
        xs2s=own_two,
        xs1r=own_all,
        xs2r=own_all,
        buf1=pltpu.VMEM((kinds, chunks, lines, rows, chunk), BF16),
        buf2=pltpu.VMEM((kinds, chunks, lines - 1, rows, chunk), BF16),
        msum=pltpu.VMEM((6, 8, model), F32),
        mtot=pltpu.VMEM((6, model), F32),
        mrecv=pltpu.VMEM((6, model), F32),
        w_sem=dma((6,)),
        in_sem=dma((11, 2)),
        gm_sem=dma((2, windows)),
        ga_sem=dma((2, windows)),
        ps1_sem=dma((2, 2)),
        ps2_sem=dma((2, 2)),
        xs1_sem=dma((2, windows)),
        xs2_sem=dma((2, windows)),
        hand_sem=dma((2, 2)),
        mod_sem=dma((2,)),
        across_sem=dma((2, kinds, chunks)),
        along_sem=dma((2, kinds, chunks, lines - 1)),
    )
    names = (*ins, *outs, *scratch)
    return pl.pallas_call(
        functools.partial(backward_kernel, windows, last, size, names),
        out_shape=[shape for shape, _ in outs.values()],
        in_specs=[spec for _, spec in ins.values()],
        out_specs=[spec for _, spec in outs.values()],
        scratch_shapes=list(scratch.values()),
        compiler_params=pltpu.CompilerParams(
            collective_id=collective_id, has_side_effects=True, vmem_limit_bytes=VMEM_LIMIT
        ),
        name="backward_last" if last else "backward_first",
    )(*[value for value, _ in ins.values()])


def lookup_kernel(index, table, out):
    heads, groups = table.shape[0], table.shape[1]
    rows, width = index.shape

    def some(r):
        for block in range(width // 128):
            c = pl.ds(block * 128, 128)
            row = index[r, c]
            low = row & 127
            high = row >> 7
            found = [jnp.zeros((16, 128), F32) for _ in range(heads)]
            for g in range(groups):
                here = high == g
                for h in range(heads):
                    spread = jnp.broadcast_to(table[h, pl.ds(g, 1), :], (16, 128))
                    taken = jnp.take_along_axis(spread, low, axis=1, mode="promise_in_bounds")
                    found[h] = jnp.where(here, taken, found[h])
            for h in range(heads):
                out[h, r, c] = found[h].astype(BF16)

    rows16(rows, some)


def bias_lookup(index, table):
    rows, heads = table.shape
    groups = (rows + 127) // 128
    spread = jnp.pad(table.astype(F32), ((0, groups * 128 - rows), (0, 0))).T
    return pl.pallas_call(
        lookup_kernel,
        out_shape=jax.ShapeDtypeStruct((heads,) + index.shape, BF16),
        name="bias_lookup",
    )(index, spread.reshape(heads, groups, 128))


def scatter(index, grad, out):
    heads = grad.shape[0]
    groups = out.shape[1] // heads
    rows, width = index.shape
    out[...] = jnp.zeros_like(out)
    low_rows = lax.broadcasted_iota(jnp.int32, (128, width), 0)
    high_rows = lax.broadcasted_iota(jnp.int32, (groups, width), 0)

    def some(rb):
        r = pl.ds(pl.multiple_of(rb * 8, 8), 8)
        index_rows = index[r, :]
        low = index_rows & 127
        high = index_rows >> 7
        grads = [grad[h, r, :] for h in range(heads)]
        total = out[...]
        for i in range(8):
            onehot = jnp.where(low_rows == low[i : i + 1], 1.0, 0.0).astype(BF16)
            here = high_rows == high[i : i + 1]
            placed = jnp.concatenate(
                [jnp.where(here, g[i : i + 1], 0.0) for g in grads], axis=0
            ).astype(BF16)
            total = total + dot_nt(onehot, placed)
        out[...] = total

    loop(rows // 8, some)


def place_index(index, layout):
    if layout == 0:
        cut, order, pad = (2, 2, 64), (1, 0, 2), 0
    else:
        cut, order, pad = (FRAMES, 2, 32), (1, 0, 2), 64
    side = index.shape[0]
    both = index.reshape(cut + cut)
    both = both.transpose(order + tuple(3 + o for o in order)).reshape(side, side)
    return jnp.pad(both, ((0, 0), (0, pad)), constant_values=-1)


def local(
    tokens,
    cond,
    pad_mask,
    spatial_index,
    joint_index,
    qkv_a,
    proj_a,
    fc1_a,
    fc2_a,
    table_a,
    ada_a,
    qkv_b,
    proj_b,
    fc1_b,
    fc2_b,
    table_b,
    ada_b,
    cotangent,
    dp_size,
    mp_size,
):
    model = tokens.shape[1]
    inner = proj_a.shape[0]
    hidden = fc1_a.shape[1]
    core = lax.rem(lax.axis_index("mp"), 2)
    params_a = (qkv_a.reshape(model, -1), proj_a, fc1_a, fc2_a)
    params_b = (qkv_b.reshape(model, -1), proj_b, fc1_b, fc2_b)

    def own_rows(values):
        whole = lax.all_gather(values, "mp", axis=0, tiled=True)
        cut = whole.reshape(2 * FRAMES, 2, 4 * SIDE, model)
        return lax.dynamic_index_in_dim(cut, core, axis=1, keepdims=False)

    cond_act = jax.nn.silu(cond.astype(F32)).astype(BF16)
    parts = jnp.concatenate(
        [jnp.dot(cond_act, ada, preferred_element_type=F32) for ada in (ada_a, ada_b)], axis=0
    )
    mods = lax.all_gather(parts, "mp", axis=1, tiled=True).reshape(2, 6, model)

    x_a = own_rows(tokens).reshape(FRAMES, -1, model)
    grad_top = own_rows(cotangent).astype(F32).reshape(FRAMES, 2, 4, 2, 8, model)
    grad_top = grad_top.transpose(1, 3, 0, 2, 4, 5).reshape(4, -1, model)

    index_a = place_index(spatial_index, 0)
    index_b = place_index(joint_index, 1)
    bias_a = bias_lookup(index_a, table_a)
    bias_b = bias_lookup(index_b, table_b)
    hidden_keys = jnp.where(pad_mask.reshape(-1) > 0, 0.0, -1e30).astype(F32)
    mask_a = hidden_keys.reshape(FRAMES, 2, 2, 64).transpose(0, 2, 1, 3).reshape(FRAMES, 1, -1)
    mask_b = hidden_keys.reshape(FRAMES, 2, 2, 4, 2, 8).transpose(1, 4, 2, 0, 3, 5)
    mask_b = mask_b.reshape(4, 1, -1)

    *kept_a, y_a = block_forward(x_a, mods[0], params_a, bias_a, mask_a, False, 1)
    x_b = y_a.reshape(4, -1, model)
    *kept_b, output = block_forward(x_b, mods[1], params_b, bias_b, mask_b, True, 2)
    grad_mid, carry, fc_b, table_grad_b, mod_b = block_backward(
        x_b, grad_top, mods[1], params_b, kept_b, index_b, table_b.shape[0], None, dp_size, 3
    )
    grad_mid = grad_mid.reshape(FRAMES, -1, model)
    grad_x, rest_b, rest_a, fc_a, table_grad_a, mod_a = block_backward(
        x_a, grad_mid, mods[0], params_a, kept_a, index_a, table_a.shape[0], carry, dp_size, 4
    )

    wide = ada_a.shape[1]
    first = lax.axis_index("mp") * wide
    mod_columns = [
        lax.dynamic_slice_in_dim(m.reshape(-1), first, wide, axis=0) for m in (mod_a, mod_b)
    ]
    small = jnp.concatenate(
        [cond_act.astype(F32).reshape(-1)]
        + mod_columns
        + [table_grad_a.reshape(-1), table_grad_b.reshape(-1)]
    )
    everyone = lax.all_gather(small, "dp", axis=0, tiled=False)
    cut = [model, model + wide, model + 2 * wide, model + 2 * wide + table_grad_a.size]
    conds, cols_a, cols_b, tables_a, tables_b = jnp.split(everyone, cut, axis=1)
    rows_here = model // dp_size
    my_conds = lax.dynamic_slice_in_dim(conds, lax.axis_index("dp") * rows_here, rows_here, axis=1)

    def outer(columns):
        return jnp.einsum("td,tc->dc", my_conds, columns, precision=HIGHEST)

    def table(parts, like, length):
        heads = table_a.shape[1]
        summed_table = jnp.sum(parts, axis=0).reshape(128, heads, -1)
        return summed_table.transpose(2, 0, 1).reshape(-1, heads)[:length]

    def split(rest, fc):
        return (
            rest[:, : 3 * inner].reshape(rows_here, 3, inner),
            rest[:, 3 * inner :].T,
            fc[0],
            fc[1].T,
        )

    return (
        output.reshape(tokens.shape),
        grad_x.reshape(tokens.shape),
        *split(rest_a, fc_a),
        table(tables_a, table_grad_a, table_a.shape[0]),
        outer(cols_a),
        *split(rest_b, fc_b),
        table(tables_b, table_grad_b, table_b.shape[0]),
        outer(cols_b),
    )


def solution(mesh):
    in_specs = (
        P(("dp", "mp"), None),
        P("dp", None),
        P("dp", None),
        P(),
        P(),
        P(None, None, "mp"),
        P("mp", None),
        P(None, "mp"),
        P("mp", None),
        P(None, "mp"),
        P(None, "mp"),
        P(None, None, "mp"),
        P("mp", None),
        P(None, "mp"),
        P("mp", None),
        P(None, "mp"),
        P(None, "mp"),
        P(("dp", "mp"), None),
    )
    out_specs = (
        P(("dp", "mp"), None),
        P(("dp", "mp"), None),
        P("dp", None, "mp"),
        P("mp", "dp"),
        P("dp", "mp"),
        P("mp", "dp"),
        P(None, "mp"),
        P("dp", "mp"),
        P("dp", None, "mp"),
        P("mp", "dp"),
        P("dp", "mp"),
        P("mp", "dp"),
        P(None, "mp"),
        P("dp", "mp"),
    )
    body = functools.partial(local, dp_size=mesh.shape["dp"], mp_size=mesh.shape["mp"])
    return jax.shard_map(body, mesh=mesh, in_specs=in_specs, out_specs=out_specs, check_vma=False)
```

time: 764 us -> 520 us (0.68); the launches traced: 763 us -> 511 us
  Pallas kernels: 637 us -> 394 us
  other arithmetic: 12 us -> 1.21 us
    pallas_call x5 -> x2, Pallas kernels: 451 us -> 236 us  [block_backward(): pl.pallas_call(functools.partial(backward_kernel, windows, last, size, na...]
    pallas_call x2, Pallas kernels: 171 us -> 143 us  [block_forward(): pl.pallas_call(functools.partial(forward_kernel, windows, last), out_shap...]
    concatenate x1 -> x0, other arithmetic: 10.8 us -> none  [local(): jnp.concatenate([weights_a, weights_b], axis=1)]
    unnamed x37 -> x43, local copies, waits for them, and re-layouts: 14.2 us -> 16.4 us
  transfers between devices with their start and end apart: 2 -> 2, of which waited for: 1 -> 1; matrix products, arithmetic and copies ran while one was open for 3% -> 4% of each run, Pallas kernels for 2% -> 3%
where the time goes in v2:
time: 520 us; the launch traced here: 511 us
  Pallas kernels  394 us (76%)
  local copies, waits for them, and re-layouts  43 us (8%)
  blocking collectives  39.1 us (8%)
  between operations  14.9 us (3%)
  waiting for transfers between devices  13.3 us (3%)
  matrix products  5.24 us (1%)
    pallas_call x2, Pallas kernels, block_backward(): pl.pallas_call(functools.partial(backward_kernel, windows, last, size, na...  236 us
    pallas_call x2, Pallas kernels, block_forward(): pl.pallas_call(functools.partial(forward_kernel, windows, last), out_shap...  143 us
    all_gather x1, blocking collectives, local(): everyone = lax.all_gather(small, 'dp', axis=0, tiled=False)  32.9 us
    unnamed x43, local copies, waits for them, and re-layouts  16.4 us
    pallas_call x2, Pallas kernels, bias_lookup(): pl.pallas_call(lookup_kernel, out_shape=jax.ShapeDtypeStruct((heads,) + i...  15 us
    all_gather x2, waiting for transfers between devices, own_rows(): whole = lax.all_gather(values, 'mp', axis=0, tiled=True)  12 us
  transfers between devices with their start and end apart: 2, of which 1 were waited for; matrix products, arithmetic and copies ran while one was open for 4% of the time, Pallas kernels for 3%

profile of v2, /device:TPU:0, one launch (start us, length us, event | category | flops | bytes accessed | tf_op | source)
XLA Modules:
  0.0 511.1 jit_solution(17184414345058644417)
XLA Ops:
  9.7 1.3 fusion.5
  12.1 6.2 %all_gather.16 = f32[2,6144]{1,0:T(2,128)S(1)} all-gather(f32[2,1536]{1,0:T(2,128)S(1)} %pad_maximum_fusion), channel_id=1, replica_groups=mesh['dp'=8,'mp'=4] {'mp'}, dimensions={1}, use_global_device_ids=true | all-gather | bytes 61440 | tf_op jit(solution)/shard_map/all_gather | solution.py:1068
  20.3 1.2 reshape.170.index.refs_2_
  23.0 1.6 copy.113.qkv_hbm.refs_14_
  26.0 2.3 reshape.176
  28.2 1.8 copy.144
  31.4 1.7 copy.116
  33.1 1.6 copy.117.qkv_hbm.refs_14_
  34.7 4.6 bias_lookup.2.bias
  40.2 10.4 %bias_lookup.3.bias = bf16[4,320,384]{2,1,0:T(8,128)(2,1)} custom-call(s32[320,384]{1,0:T(8,128)} %pad.15.index.refs_2_, f32[4,16,128]{2,1,0:T(8,128)} %bitcast.109), custom_call_target="tpu_custom_call" | custom-call | tf_op jit(solution)/shard_map/bias_lookup/pallas_call | solution.py:985
  50.6 2.5 constant_dynamic-slice_fusion.1
  53.1 11.9 %all-gather.6.cloned.1.call-done = bf16[1280,1024]{1,0:T(8,128)(2,1)} async-done(((bf16[320,1024]{1,0:T(8,128)(2,1)}), bf16[1280,1024]{1,0:T(8,128)(2,1)}) %all-gather.6.cloned.1.call-update) | async-done | bytes 2621456 | tf_op jit(solution)/shard_map/all_gather | solution.py:1060
  65.0 1.4 constant_dynamic-slice_fusion
  66.8 1.8 copy.118
  68.6 71.1 %forward_first.1 = (bf16[5,256,1024]{2,1,0:T(8,128)(2,1)}, bf16[5,256,768]{2,1,0:T(8,128)(2,1)}, bf16[5,4,256,256]{3,2,1,0:T(8,128)(2,1)}, bf16[5,256,256]{2,1,0...) custom-call(bf16[5,128,1024]{2,1,0:T(8,128)(2,1)} %bitcast.85, ...), custom_call_target="tpu_custom_call" | custom-call | tf_op jit(solution)/shard_map/forward_first/pallas_call | solution.py:395
  139.7 72.1 %forward_last.1 = (bf16[4,320,1024]{2,1,0:T(8,128)(2,1)}, bf16[4,320,768]{2,1,0:T(8,128)(2,1)}, bf16[4,4,320,320]{3,2,1,0:T(8,128)(2,1)}, bf16[4,320,256]{2,1,0:...) custom-call(f32[4,160,1024]{2,1,0:T(8,128)} %bitcast.87, ...), custom_call_target="tpu_custom_call" | custom-call | tf_op jit(solution)/shard_map/forward_last/pallas_call | solution.py:395
  211.8 107.2 %backward_last.1 = (f32[10,4,2,8,1024]{4,3,2,1,0:T(8,128)}, bf16[4,2,128,1024]{3,2,1,0:T(8,128)(2,1)}, f32[2,128,1024]{2,1,0:T(8,128)}, f32[128,64]{1,0:T(8,128)}, f32[6,1024]{1,0:T(8,128)}) custom-call(f32[4,160,1024]{2,1,0:T(8,128)} %bitcast.89, f32[6,1024]{1,0:T(8,128)} %squeeze.24.mod.refs_1_, s32[320,384]{1,0:T(8,128)} %pad.15.index.refs_2_, ...), custom_call_target="tpu_custom_call" | custom-call | tf_op jit(solution)/shard_map/backward_last/pallas_call | solution.py:945
  319.1 128.7 %backward_first.1 = (f32[5,64,1024]{2,1,0:T(8,128)}, f32[128,1024]{1,0:T(8,128)}, f32[128,1024]{1,0:T(8,128)}, f32[2,128,1024]{2,1,0:T(8,128)}, f32[128,32]{1,0:T(8,128)}, /*index=5*/f32[6,1024]{1,0:T(8,128)}) custom-call(f32[5,128,1024]{2,1,0:T(8,128)} %bitcast.98, f32[6,1024]{1,0:T(8,128)} %squeeze.23.mod.refs_1_, s32[256,256]{1,0:T(8,128)} %reshape.170.index.refs_2_, ...), custom_call_target="tpu_custom_call" | custom-call | tf_op jit(solution)/shard_map/backward_first/pallas_call | solution.py:945
  449.8 32.9 %all-gather = f32[131072]{0:T(1024)S(1)} all-gather(f32[16384]{0:T(1024)S(1)} %constant_dynamic-update-slice_fusion), channel_id=2, replica_groups=mesh['dp'=8,'mp'=4] {'dp'}, dimensions={0}, use_global_device_ids=true | all-gather | bytes 589824 | tf_op jit(solution)/shard_map/all_gather | solution.py:1104
  485.1 1.7 fusion.2
  486.8 1.7 fusion
  490.3 2.4 slice_bitcast_fusion
  498.6 2.7 copy.158
  501.3 2.5 copy.159
  (84 shorter events, 22.8 us)
Async XLA Ops:
  7.2 2.5 copy-start
  7.2 3.9 copy-start.9
  7.2 43.4 %all-gather.4.cloned.1.call-start = ((), (), s32[]{:S(2)}) async-start(), calls=%async_computation | async-start | bytes 3276800 | tf_op jit(solution)/shard_map/all_gather | solution.py:1060
  7.9 57.1 %all-gather.6.cloned.1.call-start = ((), (), s32[]{:S(2)}) async-start(), calls=%async_computation.1 | async-start | bytes 3276800 | tf_op jit(solution)/shard_map/all_gather | solution.py:1060
  9.7 1.9 copy-start.2
  9.7 10.1 %copy-start.7 = (s32[256,256]{1,0:T(8,128)S(1)}, s32[256,256]{1,0:T(8,128)}, u32[]{:S(2)}) copy-start(s32[256,256]{1,0:T(8,128)} %param.21) | copy-start | bytes 786436
  11.6 9.9 %copy-start.12 = (bf16[961,4]{0,1:T(4,128)(2,1)S(1)}, bf16[961,4]{0,1:T(4,128)(2,1)}, u32[]{:S(2)}) copy-start(bf16[961,4]{0,1:T(4,128)(2,1)} %param.27) | copy-start | bytes 23068
  11.6 10.5 %copy-start.3 = (bf16[1024,3,256]{2,0,1:T(8,128)(2,1)S(1)}, bf16[1024,3,256]{2,0,1:T(8,128)(2,1)}, u32[]{:S(2)}) copy-start(bf16[1024,3,256]{2,0,1:T(8,128)(2,1)} %param.23) | copy-start | bytes 4718596
  23.0 3.0 copy-start.6
  30.0 0.7 copy-start.11
  319.1 129.5 %copy-start.10 = (f32[6,1024]{1,0:T(8,128)S(1)}, f32[6,1024]{1,0:T(8,128)}, u32[]{:S(2)}) copy-start(f32[6,1024]{1,0:T(8,128)} %get-tuple-element.75) | copy-start | bytes 73732
  319.1 130.5 %copy-start.8 = (f32[128,64]{1,0:T(8,128)S(1)}, f32[128,64]{1,0:T(8,128)}, u32[]{:S(2)}) copy-start(f32[128,64]{1,0:T(8,128)} %get-tuple-element.77) | copy-start | bytes 98308
  447.8 36.1 %copy-start.5 = (f32[128,1024]{1,0:T(8,128)S(1)}, f32[128,1024]{1,0:T(8,128)}, u32[]{:S(2)}) copy-start(f32[128,1024]{1,0:T(8,128)} %get-tuple-element.78) | copy-start | bytes 1572868
  483.9 6.4 %copy-start.4 = (f32[2,128,1024]{2,1,0:T(8,128)S(1)}, f32[2,128,1024]{2,1,0:T(8,128)}, u32[]{:S(2)}) copy-start(f32[2,128,1024]{2,1,0:T(8,128)} %get-tuple-element.79) | copy-start | bytes 3145732
  498.6 5.2 %copy-start.1 = (bf16[1024,1536]{1,0:T(8,128)(2,1)S(1)}, bf16[1024,1536]{1,0:T(8,128)(2,1)}, u32[]{:S(2)}) copy-start(bf16[1024,1536]{1,0:T(8,128)(2,1)} %param.34) | copy-start | bytes 9437188
Sparse Core Ops, SparseCore 0:
  9.6 28.3 all-gather.3
  39.5 25.4 all-gather.5
